TPU v7x, 32 devices: a whole 2x2x4 slice. The times are simulated.
32 devices in a mesh: section: 2 (over x), batch: 16 (over z, y, core).
Axes of the slice: x: 2, y: 2, z: 4, core: 2. Of those that a mesh axis runs over, the one named last changes fastest.
Arguments:
- frames: bfloat16 [6144, 4, 84, 84], P('batch'), may hold values from 0 to 1
- next_frames: bfloat16 [6144, 4, 84, 84], P('batch'), may hold values from 0 to 1
- actions: int32 [6144], P('batch'), may hold values from 0 to 17
- next_actions: int32 [6144], P('batch'), may hold values from 0 to 17
- lengths: int32 [6144], P('batch'), may hold values from 1 to 3
- terminal: int32 [6144], P('batch'), may hold values 0 or 1
- rewards: float32 [6144, 3], P('batch'), may hold values from -1 to 1
- discounts: float32 [6144, 3], P('batch'), may hold values from 0.85 to 0.999
- owners: int32 [6144, 1], P('batch'), may hold values from 0 to 15; in each aligned block of 384 rows (0 to 383, 384 to 767, ...) at most 25 rows name the same one
- conv_one_weight: bfloat16 [32, 4, 8, 8], replicated, may hold values from -0.375 to 0.375
- conv_one_offset: bfloat16 [32], replicated, may hold values from -1 to 1
- conv_two_weight: bfloat16 [64, 32, 4, 4], replicated, may hold values from -0.25 to 0.25
- conv_two_offset: bfloat16 [64], replicated, may hold values from -1 to 1
- conv_three_weight: bfloat16 [64, 64, 3, 3], replicated, may hold values from -0.25 to 0.25
- conv_three_offset: bfloat16 [64], replicated, may hold values from -1 to 1
- dense_one_weight: bfloat16 [3136, 512], replicated, may hold values from -0.109375 to 0.109375
- dense_one_offset: bfloat16 [512], replicated, may hold values from -1 to 1
- dense_two_weight: bfloat16 [512, 918], replicated, may hold values from -0.75 to 0.75
- dense_two_offset: bfloat16 [918], replicated, may hold values from -1.5 to 1.5
- target_conv_one_weight: bfloat16 [32, 4, 8, 8], replicated, may hold values from -0.375 to 0.375
- target_conv_one_offset: bfloat16 [32], replicated, may hold values from -1 to 1
- target_conv_two_weight: bfloat16 [64, 32, 4, 4], replicated, may hold values from -0.25 to 0.25
- target_conv_two_offset: bfloat16 [64], replicated, may hold values from -1 to 1
- target_conv_three_weight: bfloat16 [64, 64, 3, 3], replicated, may hold values from -0.25 to 0.25
- target_conv_three_offset: bfloat16 [64], replicated, may hold values from -1 to 1
- target_dense_one_weight: bfloat16 [3136, 512], replicated, may hold values from -0.109375 to 0.109375
- target_dense_one_offset: bfloat16 [512], replicated, may hold values from -1 to 1
- target_dense_two_weight: bfloat16 [512, 918], replicated, may hold values from -0.75 to 0.75
- target_dense_two_offset: bfloat16 [918], replicated, may hold values from -1.5 to 1.5
Outputs:
- mean_loss: float32 [], replicated
- frames_grad: bfloat16 [6144, 4, 84, 84], P('batch', 'section')
- grad_conv_one_weight: float32 [32, 4, 8, 8], P('section')
- grad_conv_one_offset: float32 [32], P('section')
- grad_conv_two_weight: float32 [64, 32, 4, 4], P('section')
- grad_conv_two_offset: float32 [64], P('section')
- grad_conv_three_weight: float32 [64, 64, 3, 3], P('section')
- grad_conv_three_offset: float32 [64], P('section')
- grad_dense_one_weight: float32 [3136, 512], P('section')
- grad_dense_one_offset: float32 [512], P('section')
- grad_dense_two_weight: float32 [512, 918], P('section')
- grad_dense_two_offset: float32 [918], P('section')
- priority_table: float32 [16, 16, 25], P('batch', 'section')
Inputs may be any that keep to these rules, and one draw needn't show every extreme that they name: `owners`: within the transitions of one device (an aligned block of 384) no owner is named more than 25 times, a bound that some block reaches.
All inputs are finite; a program needn't handle non-finite values. No bound on the sum of `terminal` on one device may be relied on, other than what follows from the above.
Results may differ from a plain program's by a relative error of at most 0.012.
Values may be sent and summed in bfloat16 or wider, within the bound.
A program may use at most 448 MiB of HBM per device.

v0:
```python
import jax
import jax.numpy as jnp
from jax import lax
from jax.sharding import PartitionSpec as P

ACTIONS = 18
ATOMS = 51
NSTEP = 3
MICRO = 4


support_low = -10.0
support_high = 10.0


def from_behind(x, axis, by):
    count = lax.axis_size(axis)
    pairs = [(i, i + by) for i in range(count) if 0 <= i + by < count]
    return lax.ppermute(x, axis, pairs)


def as_sent(x):
    return jax.tree.map(lambda a: a.astype(jnp.bfloat16) if a.dtype == jnp.float32 else a, x)


def conv_forward(inputs, kernel, offset, stride):
    result = lax.conv_general_dilated(
        inputs,
        kernel,
        (stride, stride),
        "VALID",
        dimension_numbers=("NCHW", "OIHW", "NCHW"),
        preferred_element_type=jnp.float32,
    )
    return result + offset.astype(jnp.float32)[None, :, None, None]


def kernel_grad(inputs, cotangent, stride):
    return lax.conv_general_dilated(
        inputs,
        cotangent,
        (1, 1),
        "VALID",
        rhs_dilation=(stride, stride),
        dimension_numbers=("CNHW", "IOHW", "CNHW"),
        preferred_element_type=jnp.float32,
    )


def inputs_grad(cotangent, kernel, stride):
    extent = kernel.shape[2] - 1
    flipped = kernel[:, :, ::-1, ::-1]
    return lax.conv_general_dilated(
        cotangent,
        flipped,
        (1, 1),
        ((extent, extent), (extent, extent)),
        lhs_dilation=(stride, stride),
        dimension_numbers=("NCHW", "IOHW", "NCHW"),
        preferred_element_type=jnp.float32,
    )


def silu_slope(values):
    sigmoid = jax.nn.sigmoid(values)
    return sigmoid * (1.0 + values * (1.0 - sigmoid))


def tower_forward(inputs, weights):
    pre_one = conv_forward(inputs, weights[0], weights[1], 4)
    act_one = jax.nn.silu(pre_one).astype(jnp.bfloat16)
    pre_two = conv_forward(act_one, weights[2], weights[3], 2)
    act_two = jax.nn.silu(pre_two).astype(jnp.bfloat16)
    pre_three = conv_forward(act_two, weights[4], weights[5], 1)
    act_three = jax.nn.silu(pre_three).astype(jnp.bfloat16)
    feature = act_three.reshape(act_three.shape[0], -1)
    return (feature, (inputs, pre_one, act_one, pre_two, act_two, pre_three))


def tower_backward(feature_cot, kept, weights):
    inputs, pre_one, act_one, pre_two, act_two, pre_three = kept
    grad_three = (
        feature_cot.astype(jnp.float32).reshape(pre_three.shape) * silu_slope(pre_three)
    ).astype(jnp.bfloat16)
    back_two = inputs_grad(grad_three, weights[4], 1)
    grad_two = (back_two * silu_slope(pre_two)).astype(jnp.bfloat16)
    back_one = inputs_grad(grad_two, weights[2], 2)
    grad_one = (back_one * silu_slope(pre_one)).astype(jnp.bfloat16)
    image_grad = inputs_grad(grad_one, weights[0], 4).astype(jnp.bfloat16)
    terms = (
        kernel_grad(inputs, grad_one, 4),
        jnp.sum(grad_one, axis=(0, 2, 3), dtype=jnp.float32),
        kernel_grad(act_one, grad_two, 2),
        jnp.sum(grad_two, axis=(0, 2, 3), dtype=jnp.float32),
        kernel_grad(act_two, grad_three, 1),
        jnp.sum(grad_three, axis=(0, 2, 3), dtype=jnp.float32),
    )
    return (image_grad, terms)


def dense_forward(feature, weights):
    hidden = jnp.dot(feature, weights[0], preferred_element_type=jnp.float32) + weights[1].astype(
        jnp.float32
    )
    active = jax.nn.silu(hidden).astype(jnp.bfloat16)
    logits = jnp.dot(active, weights[2], preferred_element_type=jnp.float32) + weights[3].astype(
        jnp.float32
    )
    return (logits, hidden, active)


def pick_action(logits, chosen_ids):
    shaped = logits.reshape(logits.shape[0], ACTIONS, ATOMS)
    action_hot = (chosen_ids[:, None] == jnp.arange(ACTIONS, dtype=jnp.int32)[None, :]).astype(
        jnp.float32
    )
    return jnp.sum(shaped * action_hot[:, :, None], axis=1)


def projection(probabilities, rewards, discounts, lengths, terminal):
    step_ids = jnp.arange(NSTEP, dtype=jnp.int32)[None, :]
    inside_steps = (step_ids < lengths[:, None]).astype(jnp.float32)
    products = jnp.cumprod(discounts, axis=1)
    earlier = jnp.concatenate([jnp.ones_like(products[:, :1]), products[:, :-1]], axis=1)
    returns = jnp.sum(inside_steps * earlier * rewards, axis=1)
    final_step = (step_ids == lengths[:, None] - 1).astype(jnp.float32)
    bootstrap = jnp.sum(final_step * products, axis=1) * (1.0 - terminal.astype(jnp.float32))
    spacing = (support_high - support_low) / (ATOMS - 1)
    atom_values = support_low + spacing * jnp.arange(ATOMS, dtype=jnp.float32)
    shifted_atoms = jnp.clip(
        returns[:, None] + bootstrap[:, None] * atom_values[None, :], support_low, support_high
    )
    position = (shifted_atoms - support_low) / spacing
    weights = jnp.maximum(
        0.0,
        1.0 - jnp.abs(position[:, :, None] - jnp.arange(ATOMS, dtype=jnp.float32)[None, None, :]),
    )
    return jnp.einsum("rj,rji->ri", probabilities, weights, precision=lax.Precision.HIGHEST)


def head_step(
    feature,
    feature_next,
    action_ids,
    next_ids,
    length_ids,
    terminal_ids,
    reward_rows,
    discount_rows,
    online,
    target,
):
    logits, hidden, active = dense_forward(feature, online)
    target_logits, unused_hidden, unused_active = dense_forward(feature_next, target)
    probabilities = jax.nn.softmax(pick_action(target_logits, next_ids), axis=-1)
    mass = projection(probabilities, reward_rows, discount_rows, length_ids, terminal_ids)
    chosen = pick_action(logits, action_ids)
    row_loss = -jnp.sum(mass * jax.nn.log_softmax(chosen, axis=-1), axis=1)
    chosen_grad = jnp.sum(mass, axis=1, keepdims=True) * jax.nn.softmax(chosen, axis=-1) - mass
    action_hot = (action_ids[:, None] == jnp.arange(ACTIONS, dtype=jnp.int32)[None, :]).astype(
        jnp.float32
    )
    logit_grad = (
        (action_hot[:, :, None] * chosen_grad[:, None, :])
        .reshape(logits.shape)
        .astype(jnp.bfloat16)
    )
    hidden_back = jnp.einsum("rb,ab->ra", logit_grad, online[2], preferred_element_type=jnp.float32)
    hidden_grad = (hidden_back * silu_slope(hidden)).astype(jnp.bfloat16)
    feature_cot = jnp.einsum(
        "rh,fh->rf", hidden_grad, online[0], preferred_element_type=jnp.float32
    ).astype(jnp.bfloat16)
    terms = (
        jnp.einsum("rf,rh->fh", feature, hidden_grad, preferred_element_type=jnp.float32),
        jnp.sum(hidden_grad, axis=0, dtype=jnp.float32),
        jnp.einsum("ra,rb->ab", active, logit_grad, preferred_element_type=jnp.float32),
        jnp.sum(logit_grad, axis=0, dtype=jnp.float32),
    )
    return (feature_cot, terms, row_loss)


def silenced(function):

    def zeros_instead(*operands):
        return jax.tree.map(jnp.zeros_like, function(*operands))

    return zeros_instead


def shards(
    frames,
    next_frames,
    actions,
    next_actions,
    lengths,
    terminal,
    rewards,
    discounts,
    owners,
    conv_one_weight,
    conv_one_offset,
    conv_two_weight,
    conv_two_offset,
    conv_three_weight,
    conv_three_offset,
    dense_one_weight,
    dense_one_offset,
    dense_two_weight,
    dense_two_offset,
    target_conv_one_weight,
    target_conv_one_offset,
    target_conv_two_weight,
    target_conv_two_offset,
    target_conv_three_weight,
    target_conv_three_offset,
    target_dense_one_weight,
    target_dense_one_offset,
    target_dense_two_weight,
    target_dense_two_offset,
):
    online_tower = (
        conv_one_weight,
        conv_one_offset,
        conv_two_weight,
        conv_two_offset,
        conv_three_weight,
        conv_three_offset,
    )
    online_head = (dense_one_weight, dense_one_offset, dense_two_weight, dense_two_offset)
    target_tower = (
        target_conv_one_weight,
        target_conv_one_offset,
        target_conv_two_weight,
        target_conv_two_offset,
        target_conv_three_weight,
        target_conv_three_offset,
    )
    target_head = (
        target_dense_one_weight,
        target_dense_one_offset,
        target_dense_two_weight,
        target_dense_two_offset,
    )
    first_section = lax.axis_index("section") == 0
    row_count = frames.shape[0]
    block_rows = row_count // MICRO

    def towers(now_part, next_part):
        feature, kept = tower_forward(now_part, online_tower)
        feature_next, unused_kept = tower_forward(next_part, target_tower)
        return (feature, feature_next, kept)

    def tower_back(feature_cot, kept):
        return tower_backward(feature_cot, kept, online_tower)

    def head_work(
        arrived_now,
        arrived_later,
        action_ids,
        next_ids,
        length_ids,
        terminal_ids,
        reward_rows,
        discount_rows,
    ):
        return head_step(
            arrived_now,
            arrived_later,
            action_ids,
            next_ids,
            length_ids,
            terminal_ids,
            reward_rows,
            discount_rows,
            online_head,
            target_head,
        )

    image_grads = []
    row_losses = []
    conv_totals = None
    dense_totals = None
    for block_index in range(MICRO):
        start = block_index * block_rows
        stop = start + block_rows
        feature, feature_next, kept = lax.cond(
            first_section, towers, silenced(towers), frames[start:stop], next_frames[start:stop]
        )
        arrived, arrived_next = from_behind((feature, feature_next), "section", 1)
        feature_cot, dense_terms, row_loss = lax.cond(
            first_section,
            silenced(head_work),
            head_work,
            arrived,
            arrived_next,
            actions[start:stop],
            next_actions[start:stop],
            lengths[start:stop],
            terminal[start:stop],
            rewards[start:stop],
            discounts[start:stop],
        )
        returned = from_behind(feature_cot, "section", -1)
        image_grad, conv_terms = lax.cond(
            first_section, tower_back, silenced(tower_back), returned, kept
        )
        image_grads.append(image_grad)
        row_losses.append(row_loss)
        if block_index == 0:
            conv_totals = conv_terms
            dense_totals = dense_terms
        else:
            conv_totals = tuple((total + term for total, term in zip(conv_totals, conv_terms)))
            dense_totals = tuple((total + term for total, term in zip(dense_totals, dense_terms)))
    all_losses = jnp.concatenate(row_losses)
    owner_count = lax.axis_size("batch")
    capacity = (row_count + owner_count - 1) // owner_count + 1
    owner_ids = owners[:, 0]
    owner_hot = (owner_ids[:, None] == jnp.arange(owner_count, dtype=jnp.int32)[None, :]).astype(
        jnp.int32
    )
    ranks = jnp.sum(jnp.cumsum(owner_hot, axis=0) * owner_hot, axis=1) - 1
    outgoing = jnp.zeros((owner_count, capacity), jnp.float32).at[owner_ids, ranks].set(all_losses)
    incoming = lax.all_to_all(outgoing, "batch", split_axis=0, concat_axis=0, tiled=True)
    summed = lax.psum(
        (
            conv_totals[0],
            conv_totals[1],
            conv_totals[2],
            conv_totals[3],
            conv_totals[4],
            conv_totals[5],
            dense_totals[0],
            dense_totals[1],
            dense_totals[2],
            dense_totals[3],
        ),
        "batch",
    )
    halves = (
        lax.psum_scatter(summed[0], "section", scatter_dimension=0, tiled=True),
        lax.psum_scatter(summed[1], "section", scatter_dimension=0, tiled=True),
        lax.psum_scatter(summed[2], "section", scatter_dimension=0, tiled=True),
        lax.psum_scatter(summed[3], "section", scatter_dimension=0, tiled=True),
        lax.psum_scatter(summed[4], "section", scatter_dimension=0, tiled=True),
        lax.psum_scatter(summed[5], "section", scatter_dimension=0, tiled=True),
        lax.psum_scatter(summed[6], "section", scatter_dimension=0, tiled=True),
        lax.psum_scatter(summed[7], "section", scatter_dimension=0, tiled=True),
        lax.psum_scatter(summed[8], "section", scatter_dimension=0, tiled=True),
        lax.psum_scatter(summed[9], "section", scatter_dimension=0, tiled=True),
        lax.psum_scatter(incoming, "section", scatter_dimension=0, tiled=True),
    )
    grad_halves = halves[:10]
    table_half = halves[10]
    loss_sum = lax.psum(jnp.sum(all_losses), ("section", "batch"))
    mean_loss = loss_sum / (row_count * owner_count)
    all_image_grads = jnp.concatenate(image_grads, axis=0)
    half_stack = all_image_grads.shape[1] // 2
    upper_grads = all_image_grads[:, half_stack:]
    received_upper = from_behind(as_sent(upper_grads), "section", 1).astype(upper_grads.dtype)
    frames_grad = jnp.where(first_section, all_image_grads[:, :half_stack], received_upper)
    return (
        mean_loss,
        frames_grad,
        grad_halves[0],
        grad_halves[1],
        grad_halves[2],
        grad_halves[3],
        grad_halves[4],
        grad_halves[5],
        grad_halves[6],
        grad_halves[7],
        grad_halves[8],
        grad_halves[9],
        table_half[None],
    )


def solution(mesh):
    return jax.shard_map(
        shards,
        mesh=mesh,
        in_specs=(
            P("batch", None, None, None),
            P("batch", None, None, None),
            P("batch"),
            P("batch"),
            P("batch"),
            P("batch"),
            P("batch", None),
            P("batch", None),
            P("batch", None),
            P(),
            P(),
            P(),
            P(),
            P(),
            P(),
            P(),
            P(),
            P(),
            P(),
            P(),
            P(),
            P(),
            P(),
            P(),
            P(),
            P(),
            P(),
            P(),
            P(),
        ),
        out_specs=(
            P(),
            P("batch", "section", None, None),
            P("section", None, None, None),
            P("section"),
            P("section", None, None, None),
            P("section"),
            P("section", None, None, None),
            P("section"),
            P("section", None),
            P("section"),
            P("section", None),
            P("section"),
            P("batch", "section", None),
        ),
        check_vma=False,
    )
```

profile of v0, /device:TPU:1, one launch (start us, length us, event | category | flops | bytes accessed | tf_op | source)
XLA Modules:
  0.0 1412.5 jit_solution(7499927588958737044)
XLA Ops:
  7.2 52.8 %conditional.12 = (bf16[96,3136]{0,1:T(8,128)(2,1)}, bf16[96,3136]{0,1:T(8,128)(2,1)}, bf16[96,4,84,84]{0,1,3,2:T(4,128)(2,1)}, f32[96,32,20,20]{0,1,3,2:T(8,128...) conditional(s32[]{:T(128)} %convert_element_type.483, ...), branch_computations={%region_0.0_spmd, %region_1.2_spmd} | conditional | flops 2995470592 | bytes 48072720 | solution.py:286
  16.1 14.7 %multiply_convert_fusion.1 = (bf16[96,32,20,20]{0,1,3,2:T(8,128)(2,1)}, f32[96,32,20,20]{0,1,3,2:T(8,128)}) fusion(f32[32]{0:T(128)S(1)} %convert_element_type.345, bf16[96,4,84,84]{0,1,3,2:T(4,128)(2,1)} %slice.112, bf16[32,4,8,8]{0,3,2,1:T(8,128)(2,1)S(1)} %copy-done.11), kind=kOutput, calls=%fused_computation.4 | convolution fusion | flops 636518400 | bytes 12808320 | tf_op jit(solution)/shard_map/cond/branch_1_fun/conv_general_dilated | solution.py:27
  41.7 13.2 multiply_convert_fusion.3
  69.0 58.4 %conditional.14 = (bf16[96,3136]{0,1:T(8,128)(2,1)}, bf16[96,3136]{0,1:T(8,128)(2,1)}, bf16[96,4,84,84]{0,1,3,2:T(4,128)(2,1)}, f32[96,32,20,20]{0,1,3,2:T(8,128...) conditional(s32[]{:T(128)} %convert_element_type.483, ...), branch_computations={%region_20.22_spmd, %region_21.23_spmd} | conditional | flops 2995470592 | bytes 46825180 | solution.py:286
  78.8 14.5 %multiply_convert_fusion.10 = (bf16[96,32,20,20]{0,1,3,2:T(8,128)(2,1)}, f32[96,32,20,20]{0,1,3,2:T(8,128)}) fusion(f32[32]{0:T(128)S(1)} %convert_element_type.372, bf16[96,4,84,84]{0,1,3,2:T(4,128)(2,1)} %slice.121, bf16[32,4,8,8]{0,3,2,1:T(8,128)(2,1)S(1)} %get-tuple-element.1849), kind=kOutput, calls=%fused_computation.21 | convolution fusion | flops 636518400 | bytes 12808320 | tf_op jit(solution)/shard_map/cond/branch_1_fun/conv_general_dilated | solution.py:27
  105.0 17.2 %multiply_convert_fusion.12 = bf16[96,64,9,9]{0,1,3,2:T(8,128)(2,1)} fusion(f32[32]{0:T(128)S(1)} %convert_element_type.378, f32[64]{0:T(128)S(1)} %convert_element_type.380, bf16[384,4,84,84]{0,1,3,2:T(4,128)(2,1)} %get-tuple-element.390, bf16[64,32,4,4]{0,3,2,1:T(4,128)(2,1)S(1)} %get-tuple-element.1858, bf16[32,4,8,8]{0,3,2,1:T(8,128)(2,1)S(1)} %get-tuple-element.1856), kind=kOutput, calls=%fused_computation.24 | convolution fusion | flops 1149112320 | bytes 8302976 | tf_op jit(solution)/shard_map/cond/branch_1_fun/conv_general_dilated | solution.py:27
  136.9 57.2 %conditional.16 = (bf16[96,3136]{0,1:T(8,128)(2,1)}, bf16[96,3136]{0,1:T(8,128)(2,1)}, bf16[96,4,84,84]{0,1,3,2:T(4,128)(2,1)}, f32[96,32,20,20]{0,1,3,2:T(8,128...) conditional(s32[]{:T(128)} %convert_element_type.483, ...), branch_computations={%region_38.40_spmd, %region_39.41_spmd} | conditional | flops 2995470592 | bytes 46826004 | solution.py:286
  146.6 14.5 %multiply_convert_fusion.19 = (bf16[96,32,20,20]{0,1,3,2:T(8,128)(2,1)}, f32[96,32,20,20]{0,1,3,2:T(8,128)}) fusion(f32[32]{0:T(128)S(1)} %convert_element_type.399, bf16[96,4,84,84]{0,1,3,2:T(4,128)(2,1)} %slice.130, bf16[32,4,8,8]{0,3,2,1:T(8,128)(2,1)S(1)} %get-tuple-element.1879), kind=kOutput, calls=%fused_computation.38 | convolution fusion | flops 636518400 | bytes 12808320 | tf_op jit(solution)/shard_map/cond/branch_1_fun/conv_general_dilated | solution.py:27
  171.6 17.3 %multiply_convert_fusion.21 = bf16[96,64,9,9]{0,1,3,2:T(8,128)(2,1)} fusion(f32[32]{0:T(128)S(1)} %convert_element_type.405, f32[64]{0:T(128)S(1)} %convert_element_type.407, bf16[384,4,84,84]{0,1,3,2:T(4,128)(2,1)} %get-tuple-element.420, bf16[64,32,4,4]{0,3,2,1:T(4,128)(2,1)S(1)} %get-tuple-element.1888, bf16[32,4,8,8]{0,3,2,1:T(8,128)(2,1)S(1)} %get-tuple-element.1886), kind=kOutput, calls=%fused_computation.41 | convolution fusion | flops 1149112320 | bytes 8302976 | tf_op jit(solution)/shard_map/cond/branch_1_fun/conv_general_dilated | solution.py:27
  203.4 63.4 %conditional.18 = (bf16[96,3136]{0,1:T(8,128)(2,1)}, bf16[96,3136]{0,1:T(8,128)(2,1)}, bf16[96,4,84,84]{0,1,3,2:T(4,128)(2,1)}, f32[96,32,20,20]{0,1,3,2:T(8,128...) conditional(s32[]{:T(128)} %convert_element_type.483, ...), branch_computations={%region_56.58_spmd, %region_57.59_spmd} | conditional | flops 2995470592 | bytes 47432624 | solution.py:286
  214.2 14.6 %multiply_convert_fusion.28 = (bf16[96,32,20,20]{0,1,3,2:T(8,128)(2,1)}, f32[96,32,20,20]{0,1,3,2:T(8,128)}) fusion(f32[32]{0:T(128)S(1)} %convert_element_type.426, bf16[96,4,84,84]{0,1,3,2:T(4,128)(2,1)} %slice.139, bf16[32,4,8,8]{0,3,2,1:T(8,128)(2,1)S(1)} %get-tuple-element.1909), kind=kOutput, calls=%fused_computation.55 | convolution fusion | flops 636518400 | bytes 12808320 | tf_op jit(solution)/shard_map/cond/branch_1_fun/conv_general_dilated | solution.py:27
  245.0 14.4 %multiply_convert_fusion.30 = bf16[96,64,9,9]{0,1,3,2:T(8,128)(2,1)} fusion(f32[32]{0:T(128)} %convert_element_type.432, f32[64]{0:T(128)} %convert_element_type.434, bf16[384,4,84,84]{0,1,3,2:T(4,128)(2,1)} %get-tuple-element.450, bf16[64,32,4,4]{0,3,2,1:T(4,128)(2,1)S(1)} %get-tuple-element.1918, bf16[32,4,8,8]{0,3,2,1:T(8,128)(2,1)} %get-tuple-element.1916), kind=kOutput, calls=%fused_computation.58 | convolution fusion | flops 1149112320 | bytes 8352768 | tf_op jit(solution)/shard_map/cond/branch_1_fun/conv_general_dilated | solution.py:27
  307.3 117.1 %conditional.20 = (bf16[96,4,84,84]{0,1,3,2:T(4,128)(2,1)S(1)}, f32[32]{0:T(128)S(1)}, f32[64,32,4,4]{0,1,3,2:T(8,128)S(1)}, f32[64]{0:T(128)S(1)}, f32[64]{0:T(...) conditional(s32[]{:T(128)} %convert_element_type.483, () %tuple.118, ...), branch_computations={%region_75.77_spmd, %region_76.81_spmd} | conditional | flops 2996152320 | bytes 39871216 | solution.py:304
  325.8 76.7 %convolution_convert_fusion = bf16[96,4,84,84]{0,1,3,2:T(4,128)(2,1)S(1)} fusion(bf16[96,32,20,20]{0,1,3,2:T(8,128)(2,1)S(1)} %get-tuple-element.2079, bf16[32,4,8,8]{0,3,2,1:T(8,128)(2,1)S(1)} %get-tuple-element.1944), kind=kOutput, calls=%fused_computation.69 | convolution fusion | flops 631855104 | bytes 7892992 | tf_op jit(solution)/shard_map/cond/branch_1_fun/conv_general_dilated | solution.py:53
  402.6 11.8 fusion.157
  427.6 118.6 %conditional.21 = (bf16[96,4,84,84]{0,1,3,2:T(4,128)(2,1)}, f32[32]{0:T(128)S(1)}, f32[64,32,4,4]{0,1,3,2:T(8,128)S(1)}, f32[64]{0:T(128)S(1)}, f32[64]{0:T(128)...) conditional(s32[]{:T(128)} %convert_element_type.483, () %tuple.120, ...), branch_computations={%region_80.82_spmd, %region_81.86_spmd} | conditional | flops 2996152320 | bytes 39871216 | solution.py:304
  446.2 78.2 %convolution_convert_fusion.1 = bf16[96,4,84,84]{0,1,3,2:T(4,128)(2,1)} fusion(bf16[96,32,20,20]{0,1,3,2:T(8,128)(2,1)S(1)} %get-tuple-element.2083, bf16[32,4,8,8]{0,3,2,1:T(8,128)(2,1)S(1)} %get-tuple-element.1954), kind=kOutput, calls=%fused_computation.89 | convolution fusion | flops 631855104 | bytes 7892992 | tf_op jit(solution)/shard_map/cond/branch_1_fun/conv_general_dilated | solution.py:53
  524.4 11.8 fusion.159
  546.9 117.1 %conditional.22 = (bf16[96,4,84,84]{0,1,3,2:T(4,128)(2,1)S(1)}, f32[32]{0:T(128)S(1)}, f32[64,32,4,4]{0,1,3,2:T(8,128)S(1)}, f32[64]{0:T(128)S(1)}, f32[64]{0:T(...) conditional(s32[]{:T(128)} %convert_element_type.483, () %tuple.122, ...), branch_computations={%region_85.87_spmd, %region_86.91_spmd} | conditional | flops 2996152320 | bytes 39871216 | solution.py:304
  565.5 76.7 %convolution_convert_fusion.2 = bf16[96,4,84,84]{0,1,3,2:T(4,128)(2,1)S(1)} fusion(bf16[96,32,20,20]{0,1,3,2:T(8,128)(2,1)S(1)} %get-tuple-element.2087, bf16[32,4,8,8]{0,3,2,1:T(8,128)(2,1)S(1)} %get-tuple-element.1964), kind=kOutput, calls=%fused_computation.109 | convolution fusion | flops 631855104 | bytes 7892992 | tf_op jit(solution)/shard_map/cond/branch_1_fun/conv_general_dilated | solution.py:53
  642.2 11.8 fusion.161
  667.2 119.1 %conditional.23 = (bf16[96,4,84,84]{0,1,3,2:T(4,128)(2,1)}, f32[32]{0:T(128)S(1)}, f32[64,32,4,4]{0,1,3,2:T(8,128)S(1)}, f32[64]{0:T(128)S(1)}, f32[64]{0:T(128)...) conditional(s32[]{:T(128)} %convert_element_type.483, () %tuple.124, (bf16[96,3136]{1,0:T(8,128)(2,1)}, ...), branch_computations={%region_90.92_spmd, %region_91.96_spmd} | conditional | flops 2996152320 | bytes 39871216 | solution.py:304
  685.7 78.2 %convolution_convert_fusion.3 = bf16[96,4,84,84]{0,1,3,2:T(4,128)(2,1)} fusion(bf16[96,32,20,20]{0,1,3,2:T(8,128)(2,1)S(1)} %get-tuple-element.2091, bf16[32,4,8,8]{0,3,2,1:T(8,128)(2,1)S(1)} %get-tuple-element.1974), kind=kOutput, calls=%fused_computation.129 | convolution fusion | flops 631855104 | bytes 7892992 | tf_op jit(solution)/shard_map/cond/branch_1_fun/conv_general_dilated | solution.py:53
  763.9 11.8 fusion.163
  797.4 12.8 add_add_fusion
  810.2 42.6 %pad_maximum_fusion = bf16[384,4,84,84]{0,1,3,2:T(4,128)(2,1)} fusion(bf16[96,4,84,84]{0,1,3,2:T(4,128)(2,1)} %get-tuple-element.653, bf16[96,4,84,84]{0,1,3,2:T(4,128)(2,1)} %copy-done.2, bf16[96,4,84,84]{0,1,3,2:T(4,128)(2,1)} %get-tuple-element.637, bf16[96,4,84,84]{0,1,3,2:T(4,128)(2,1)} %copy-done.1), kind=kLoop, calls=%fused_computation.313 | loop fusion | flops 86704128 | bytes 43352064 | tf_op jit(solution)/shard_map/concatenate | solution.py:357
  852.9 14.6 %slice.159 = bf16[384,2,84,84]{0,1,3,2:T(2,128)(2,1)} slice(bf16[384,4,84,84]{0,1,3,2:T(4,128)(2,1)} %pad_maximum_fusion), slice={[0:384], [2:4], [0:84], [0:84]} | slice | bytes 21676032 | tf_op jit(solution)/shard_map/slice | solution.py:359
  878.8 53.9 %scatter_fusion = f32[16,25]{1,0:T(8,128)} fusion(f32[16,25]{1,0:T(8,128)} %broadcast_in_dim.4, s32[384]{0:T(512)S(1)} %fusion.148, f32[384]{0:T(512)S(1)} %pad_maximum_fusion.1), kind=kCustom, calls=%fused_computation | custom fusion | bytes 7680 | tf_op jit(solution)/shard_map/scatter | solution.py:323
  940.2 269.7 %psum.77 = f32[]{:T(128)} all-reduce(f32[]{:T(128)S(6)} %reduce_sum.533), channel_id=1, replica_groups=mesh['section'=2,'batch'=16] {'section','batch'}, use_global_device_ids=true, to_apply=%region_74.76 | all-reduce | flops 1 | bytes 8 | tf_op jit(solution)/shard_map/psum | solution.py:355
  1218.0 59.5 %all-reduce.11 = (f32[16,4,8,8]{0,3,2,1:T(8,128)}, f32[16]{0:T(128)}, f32[32]{0:T(128)}, f32[32]{0:T(128)}, f32[256]{0:T(256)}, /*index=5*/f32[459]{0:T(512)}) all-reduce(f32[16,4,8,8]{0,3,2,1:T(8,128)S(1)} %bitcast.192, f32[16]{0:T(128)S(1)} %dynamic-slice.1, ...), channel_id=1, replica_groups=mesh['section'=2,'batch'=16] {'batch'}, use_global_device_ids=true, to_apply=%region_95.97 | all-reduce | flops 4891 | bytes 39128 | tf_op jit(solution)/shard_map/psum | solution.py:325
  1279.2 14.1 broadcast_select_fusion
  1293.3 102.6 %all-reduce.19.cloned.1.call-done = (f32[32,32,4,4]{1,3,2,0:T(4,128)}, f32[32,64,3,3]{1,0,3,2:T(8,128)}, f32[1568,512]{1,0:T(8,128)}, f32[256,918]{0,1:T(8,128)}) async-done(((f32[32,32,4,4]{1,3,2,0:T(4,128)}, f32[32,64,3,3]{1,0,3,2:T(8,128)}, f32[1568,512]{1,0:T(8,128)}, f32[256,918]{0,1:T(8,128)}), (f32[32,32,4,4]{1,3,2,0:T(4,128)}, f32[32,64,3,3]{1,0,3,2:T(8,128)}, f32[1568,512]{1,0:T(8,128)}, ...) | async-done | bytes 4290576 | tf_op jit(solution)/shard_map/psum | solution.py:325
  (391 shorter events, 364.0 us)
Async XLA Ops:
  7.2 1210.0 %reduce-scatter.13.cloned.1.call-start = ((), (), s32[]{:S(2)}) async-start(), calls=%async_computation.8 | async-start | bytes 49152
  62.4 138.9 %collective-permute-start = (bf16[96,3136]{1,0:T(8,128)(2,1)S(1)}, bf16[96,3136]{1,0:T(8,128)(2,1)}, u32[]{:S(2)}, u32[]{:S(2)}) collective-permute-start(bf16[96,3136]{1,0:T(8,128)(2,1)S(1)} %copy.657), channel_id=1, source_target_pairs={{0,16},{1,17},{2,18},{3,19},{4,20},{5,21},{6,22},{7,23},{8,24},{9,... | collective-permute-start | bytes 1806344 | tf_op jit(solution)/shard_map/ppermute | solution.py:19
  66.8 204.6 %collective-permute-start.1 = (bf16[96,3136]{1,0:T(8,128)(2,1)}, bf16[96,3136]{1,0:T(8,128)(2,1)}, u32[]{:S(2)}, u32[]{:S(2)}) collective-permute-start(bf16[96,3136]{1,0:T(8,128)(2,1)} %copy.658), channel_id=1, source_target_pairs={{0,16},{1,17},{2,18},{3,19},{4,20},{5,21},{6,22},{7,23},{8,24},{9,... | collective-permute-start | bytes 1806344 | tf_op jit(solution)/shard_map/ppermute | solution.py:19
  130.4 143.2 %collective-permute-start.2 = (bf16[96,3136]{1,0:T(8,128)(2,1)}, bf16[96,3136]{1,0:T(8,128)(2,1)}, u32[]{:S(2)}, u32[]{:S(2)}) collective-permute-start(bf16[96,3136]{1,0:T(8,128)(2,1)} %copy.665), channel_id=1, source_target_pairs={{0,16},{1,17},{2,18},{3,19},{4,20},{5,21},{6,22},{7,23},{8,24},{9,... | collective-permute-start | bytes 1806344 | tf_op jit(solution)/shard_map/ppermute | solution.py:19
  134.7 147.0 %collective-permute-start.3 = (bf16[96,3136]{1,0:T(8,128)(2,1)}, bf16[96,3136]{1,0:T(8,128)(2,1)}, u32[]{:S(2)}, u32[]{:S(2)}) collective-permute-start(bf16[96,3136]{1,0:T(8,128)(2,1)} %copy.666), channel_id=1, source_target_pairs={{0,16},{1,17},{2,18},{3,19},{4,20},{5,21},{6,22},{7,23},{8,24},{9,... | collective-permute-start | bytes 1806344 | tf_op jit(solution)/shard_map/ppermute | solution.py:19
  196.9 92.2 %collective-permute-start.4 = (bf16[96,3136]{1,0:T(8,128)(2,1)}, bf16[96,3136]{1,0:T(8,128)(2,1)}, u32[]{:S(2)}, u32[]{:S(2)}) collective-permute-start(bf16[96,3136]{1,0:T(8,128)(2,1)} %copy.673), channel_id=1, source_target_pairs={{0,16},{1,17},{2,18},{3,19},{4,20},{5,21},{6,22},{7,23},{8,24},{9,... | collective-permute-start | bytes 1806344 | tf_op jit(solution)/shard_map/ppermute | solution.py:19
  201.3 89.2 %collective-permute-start.5 = (bf16[96,3136]{1,0:T(8,128)(2,1)}, bf16[96,3136]{1,0:T(8,128)(2,1)}, u32[]{:S(2)}, u32[]{:S(2)}) collective-permute-start(bf16[96,3136]{1,0:T(8,128)(2,1)} %copy.674), channel_id=1, source_target_pairs={{0,16},{1,17},{2,18},{3,19},{4,20},{5,21},{6,22},{7,23},{8,24},{9,... | collective-permute-start | bytes 1806344 | tf_op jit(solution)/shard_map/ppermute | solution.py:19
  271.4 26.2 %collective-permute-start.6 = (bf16[96,3136]{1,0:T(8,128)(2,1)}, bf16[96,3136]{1,0:T(8,128)(2,1)}, u32[]{:S(2)}, u32[]{:S(2)}) collective-permute-start(bf16[96,3136]{1,0:T(8,128)(2,1)} %copy.681), channel_id=1, source_target_pairs={{0,16},{1,17},{2,18},{3,19},{4,20},{5,21},{6,22},{7,23},{8,24},{9,... | collective-permute-start | bytes 1806344 | tf_op jit(solution)/shard_map/ppermute | solution.py:19
  273.6 26.0 %collective-permute-start.7 = (bf16[96,3136]{1,0:T(8,128)(2,1)}, bf16[96,3136]{1,0:T(8,128)(2,1)}, u32[]{:S(2)}, u32[]{:S(2)}) collective-permute-start(bf16[96,3136]{1,0:T(8,128)(2,1)} %copy.682), channel_id=1, source_target_pairs={{0,16},{1,17},{2,18},{3,19},{4,20},{5,21},{6,22},{7,23},{8,24},{9,... | collective-permute-start | bytes 1806344 | tf_op jit(solution)/shard_map/ppermute | solution.py:19
  281.7 25.5 %collective-permute-start.8 = (bf16[96,3136]{1,0:T(8,128)(2,1)}, bf16[96,3136]{1,0:T(8,128)(2,1)}, u32[]{:S(2)}, u32[]{:S(2)}) collective-permute-start(bf16[96,3136]{1,0:T(8,128)(2,1)} %get-tuple-element.622), channel_id=1, source_target_pairs={{16,0},{17,1},{18,2},{19,3},{20,4},{21,5},{22,6},{23,7},{24,8},{25... | collective-permute-start | bytes 1806344 | tf_op jit(solution)/shard_map/ppermute | solution.py:19
  289.1 135.3 %collective-permute-start.9 = (bf16[96,3136]{1,0:T(8,128)(2,1)}, bf16[96,3136]{1,0:T(8,128)(2,1)}, u32[]{:S(2)}, u32[]{:S(2)}) collective-permute-start(bf16[96,3136]{1,0:T(8,128)(2,1)} %get-tuple-element.630), channel_id=1, source_target_pairs={{16,0},{17,1},{18,2},{19,3},{20,4},{21,5},{22,6},{23,7},{24,8},{25... | collective-permute-start | bytes 1806344 | tf_op jit(solution)/shard_map/ppermute | solution.py:19
  296.3 249.9 %collective-permute-start.10 = (bf16[96,3136]{1,0:T(8,128)(2,1)}, bf16[96,3136]{1,0:T(8,128)(2,1)}, u32[]{:S(2)}, u32[]{:S(2)}) collective-permute-start(bf16[96,3136]{1,0:T(8,128)(2,1)} %get-tuple-element.638), channel_id=1, source_target_pairs={{16,0},{17,1},{18,2},{19,3},{20,4},{21,5},{22,6},{23,7},{24,8},{25... | collective-permute-start | bytes 1806344 | tf_op jit(solution)/shard_map/ppermute | solution.py:19
  305.9 358.2 %collective-permute-start.11 = (bf16[96,3136]{1,0:T(8,128)(2,1)}, bf16[96,3136]{1,0:T(8,128)(2,1)}, u32[]{:S(2)}, u32[]{:S(2)}) collective-permute-start(bf16[96,3136]{1,0:T(8,128)(2,1)} %get-tuple-element.646), channel_id=1, source_target_pairs={{16,0},{17,1},{18,2},{19,3},{20,4},{21,5},{22,6},{23,7},{24,8},{25... | collective-permute-start | bytes 1806344 | tf_op jit(solution)/shard_map/ppermute | solution.py:19
  425.1 121.1 %copy-start.10 = (bf16[32,4,8,8]{0,3,2,1:T(8,128)(2,1)S(1)}, bf16[32,4,8,8]{0,3,2,1:T(8,128)(2,1)}, u32[]{:S(2)}) copy-start(bf16[32,4,8,8]{0,3,2,1:T(8,128)(2,1)} %param.63) | copy-start | bytes 49156
  788.2 489.3 %all-reduce.17.cloned.1.call-start = ((), (), s32[]{:S(2)}) async-start(), calls=%async_computation.9 | async-start | bytes 1048576
  790.6 488.5 %reduce-scatter.7.cloned.1.call-start = ((), (), s32[]{:S(2)}) async-start(), calls=%async_computation.5 | async-start | bytes 442368 | tf_op jit(solution)/shard_map/reduce_scatter | solution.py:345
  792.4 486.7 %reduce-scatter.11.cloned.1.call-start = ((), (), s32[]{:S(2)}) async-start(), calls=%async_computation.7 | async-start | bytes 2826240 | tf_op jit(solution)/shard_map/reduce_scatter | solution.py:349
  797.3 481.8 %reduce-scatter.9.cloned.1.call-start = ((), (), s32[]{:S(2)}) async-start(), calls=%async_computation.6 | async-start | bytes 9633792 | tf_op jit(solution)/shard_map/reduce_scatter | solution.py:347
  867.5 343.0 %copy-start.53 = (f32[512]{0:T(512)S(1)}, f32[512]{0:T(512)}, u32[]{:S(2)}) copy-start(f32[512]{0:T(512)} %copy-done.52) | copy-start | bytes 6148
  867.5 343.0 %copy-start.55 = (f32[512]{0:T(512)S(1)}, f32[512]{0:T(512)}, u32[]{:S(2)}) copy-start(f32[512]{0:T(512)} %copy-done.54) | copy-start | bytes 6148
  867.5 343.0 %copy-start.57 = (f32[512]{0:T(512)S(1)}, f32[512]{0:T(512)}, u32[]{:S(2)}) copy-start(f32[512]{0:T(512)} %copy-done.56) | copy-start | bytes 6148
  867.5 343.0 %copy-start.59 = (f32[512]{0:T(512)S(1)}, f32[512]{0:T(512)}, u32[]{:S(2)}) copy-start(f32[512]{0:T(512)} %copy-done.58) | copy-start | bytes 6148
  867.6 343.1 %copy-start.44 = (f32[918]{0:T(1024)S(1)}, f32[918]{0:T(1024)}, u32[]{:S(2)}) copy-start(f32[918]{0:T(1024)} %copy-done.43) | copy-start | bytes 11020
  867.6 343.1 %copy-start.46 = (f32[918]{0:T(1024)S(1)}, f32[918]{0:T(1024)}, u32[]{:S(2)}) copy-start(f32[918]{0:T(1024)} %copy-done.45) | copy-start | bytes 11020
  867.6 343.1 %copy-start.48 = (f32[918]{0:T(1024)S(1)}, f32[918]{0:T(1024)}, u32[]{:S(2)}) copy-start(f32[918]{0:T(1024)} %copy-done.47) | copy-start | bytes 11020
  867.6 343.1 %copy-start.50 = (f32[918]{0:T(1024)S(1)}, f32[918]{0:T(1024)}, u32[]{:S(2)}) copy-start(f32[918]{0:T(1024)} %copy-done.49) | copy-start | bytes 11020
  867.6 343.1 %copy-start.66 = (f32[64]{0:T(128)S(1)}, f32[64]{0:T(128)}, u32[]{:S(2)}) copy-start(f32[64]{0:T(128)} %copy-done.65) | copy-start | bytes 772
  867.6 343.1 %copy-start.68 = (f32[64]{0:T(128)S(1)}, f32[64]{0:T(128)}, u32[]{:S(2)}) copy-start(f32[64]{0:T(128)} %copy-done.67) | copy-start | bytes 772
  867.6 343.1 %copy-start.64 = (f32[32]{0:T(128)S(1)}, f32[32]{0:T(128)}, u32[]{:S(2)}) copy-start(f32[32]{0:T(128)} %copy-done.63) | copy-start | bytes 388
  867.6 411.5 %collective-permute-start.12 = (bf16[384,2,84,84]{0,1,3,2:T(2,128)(2,1)}, bf16[384,2,84,84]{0,1,3,2:T(2,128)(2,1)}, u32[]{:S(2)}, u32[]{:S(2)}) collective-permute-start(bf16[384,2,84,84]{0,1,3,2:T(2,128)(2,1)} %slice.159), channel_id=1, source_target_pairs={{0,16},{1,17},{2,18},{3,19},{4,20},{5,21},{6,22},{7,23},{8,24},{9,... | collective-permute-start | bytes 32514056 | tf_op jit(solution)/shard_map/ppermute | solution.py:19
  932.8 277.9 %all-to-all-start = ((f32[16,1,25]{2,1,0:T(1,128)}), f32[16,1,25]{2,1,0:T(1,128)S(1)}, u32[]{:S(2)}, u32[]{:S(2)}) async-start(f32[16,1,25]{2,1,0:T(1,128)} %bitcast.6), calls=%async_computation | async-start | bytes 16384 | tf_op jit(solution)/shard_map/all_to_all | solution.py:324
  940.1 455.8 %all-reduce.19.cloned.1.call-start = ((), (), s32[]{:S(2)}) async-start(), calls=%async_computation.10 | async-start | bytes 9125888 | tf_op jit(solution)/shard_map/psum | solution.py:325
  (82 other events, 654.0 us)
Sparse Core Ops, SparseCore 0:
  788.3 10.4 reduce-scatter.12
  801.7 29.0 all-reduce.16
  833.1 12.0 reduce-scatter.6
  847.9 30.5 reduce-scatter.10
  880.7 146.7 reduce-scatter.8
  1279.3 116.5 all-reduce.18
where the time goes:
time: 1420 us; the launch traced here: 1410 us
  matrix products  618 us (44%)
  blocking collectives  335 us (24%)
  local copies, waits for them, and re-layouts  197 us (14%)
  waiting for transfers between devices  105 us (7%)
  other arithmetic  98.1 us (7%)
  starting transfers between devices  35 us (2%)
  between operations  20.6 us (1%)
    conv_general_dilated x12, matrix products, inputs_grad(): lax.conv_general_dilated(cotangent, flipped, (1, 1), ((extent, extent), (...  364 us
    psum x1, blocking collectives, shards(): loss_sum = lax.psum(jnp.sum(all_losses), ('section', 'batch'))  270 us
    conv_general_dilated x20, matrix products, conv_forward(): lax.conv_general_dilated(inputs, kernel, (stride, stride), 'VALID', dimen...  168 us
    psum x1, waiting for transfers between devices, shards(): lax.psum((conv_totals[0], conv_totals[1], conv_totals[2], conv_totals[3],...  103 us
    conv_general_dilated x8, matrix products, kernel_grad(): lax.conv_general_dilated(inputs, cotangent, (1, 1), 'VALID', rhs_dilation...  66.6 us
    psum x1, blocking collectives, shards(): lax.psum((conv_totals[0], conv_totals[1], conv_totals[2], conv_totals[3],...  59.5 us
    scatter x1, local copies, waits for them, and re-layouts, shards(): jnp.zeros((owner_count, capacity), jnp.float32).at[owner_ids, ranks]  53.9 us
    concatenate x1, other arithmetic, shards(): all_image_grads = jnp.concatenate(image_grads, axis=0)  42.6 us
  transfers between devices with their start and end apart: 20, of which 2 were waited for; matrix products, arithmetic and copies ran while one was open for 51% of the time, Pallas kernels for 0%

commit v1 on v0

v1 whole, which is shorter than its diff:
```python
import functools

import jax
import jax.numpy as jnp
import numpy as np
from jax import lax
from jax.experimental import pallas as pl
from jax.experimental.pallas import tpu as pltpu
from jax.sharding import PartitionSpec as P

ACTIONS = 18
ATOMS = 51
NSTEP = 3
LANES = 128
SLICE = 32
ROW_CHUNKS = ((0, 36), (36, 84))
MESH = pl.DeviceIdType.MESH
support_low = -10.0
support_high = 10.0
F32 = jnp.float32
BF16 = jnp.bfloat16
NT = (((1,), (1,)), ((), ()))


def nn_dot(a, b):
    return jnp.dot(a, b, preferred_element_type=F32)


def nt_dot(a, b):
    return lax.dot_general(a, b, NT, preferred_element_type=F32)


def stack(parts):
    return jnp.concatenate(parts, axis=0)


def beside(parts):
    return jnp.concatenate(parts, axis=1)


def eye(size):
    rows = lax.broadcasted_iota(jnp.int32, (size, size), 0)
    cols = lax.broadcasted_iota(jnp.int32, (size, size), 1)
    return jnp.where(rows == cols, 1.0, 0.0).astype(BF16)


def order_rows(channels, extent):
    count = channels * extent * extent
    chosen = np.zeros((count, count), np.float32)
    for c in range(channels):
        for u in range(extent):
            for v in range(extent):
                chosen[(u * extent + v) * channels + c, (c * extent + u) * extent + v] = 1.0
    return jnp.asarray(chosen, BF16)


def back_one_choice():
    chosen = np.zeros((2, 8, 4, 28, 2, 128), np.float32)
    for dp in range(2):
        for dq in range(8):
            for i in range(4):
                for x in range(28):
                    u, v = i + 4 * (1 - dp), x + 4 - 4 * dq
                    if 0 <= v < 8:
                        for ch in range(2):
                            chosen[dp, dq, i, x, ch, ch * 64 + u * 8 + v] = 1.0
    return jnp.asarray(chosen.reshape(16 * 224, 128), BF16)


def lane_bias(row, size):
    return nt_dot(eye(size), jnp.broadcast_to(row, (LANES, size)))


def activate(h):
    t = jnp.tanh(h)
    m = h * t
    return h + m, (1.0 + t) * ((1.0 + h) - m)


def in_turn(jobs):
    waiting = None
    for first, then in jobs:
        value = first()
        if waiting is not None:
            waiting[0](waiting[1])
        waiting = (then, value)
    waiting[0](waiting[1])


def whole(shape):
    return pl.BlockSpec(shape, lambda i, *_: (0,) * len(shape))


def by_lane(shape):
    return pl.BlockSpec(shape[:-1] + (LANES,), lambda i, *_: (0,) * (len(shape) - 1) + (i,))


def lane_column(row):
    size = row.shape[1]
    parts = []
    for at in range(0, size, LANES):
        step = min(LANES, size - at)
        parts.append(lane_bias(row[:, at : at + step], step))
    return stack(parts)


def softmax_terms(v):
    top = jnp.max(v, axis=0, keepdims=True)
    e = jnp.exp(v - top)
    total = jnp.sum(e, axis=0, keepdims=True)
    return e / total, v - top - jnp.log(total)


def head_kernel(
    x_any,
    y_any,
    dense_any,
    target_dense_any,
    w1_ref,
    w2_ref,
    w3_ref,
    o1_ref,
    o2_ref,
    o3_ref,
    v1_ref,
    v2_ref,
    v3_ref,
    q1_ref,
    q2_ref,
    q3_ref,
    p1_ref,
    p2_ref,
    out_ref,
    target_out_ref,
    b1_ref,
    d1_ref,
    action_ref,
    later_action_ref,
    length_ref,
    terminal_ref,
    b2_ref,
    d2_ref,
    rewards_ref,
    discounts_ref,
    a1_any,
    s1_any,
    a2_any,
    s2_any,
    s3_any,
    f_any,
    active_ref,
    lg_ref,
    hg_ref,
    loss_ref,
    sum1_ref,
    sum2_ref,
    wt1,
    wt2,
    wt3,
    wt4,
    c1,
    c2,
    c3,
    c4,
    fs,
    fb,
    xbuf,
    a1,
    s1,
    a2,
    s2,
    s3,
    wd,
    wdt,
    pre,
    hidden,
    late,
    back,
    logits,
    logits_later,
    lgs,
    probs,
    position,
    x_sems,
    out_sems,
    wd_sem,
    sent,
    came,
):
    section, batch = lax.axis_index("section"), lax.axis_index("batch")
    step, steps = pl.program_id(0), pl.num_programs(0)
    lanes = hidden.shape[1]
    tiles = lanes // LANES
    targets = tiles - 1
    online = step >= targets
    slot = lax.rem(step, 2)
    height, width, stacked, _ = x_any.shape

    def lanes_of(index):
        return pl.ds(pl.multiple_of(index * LANES, LANES), LANES)

    def x_copy(source, tile, at, k):
        place = lax.rem(at, 2)
        first, last = ROW_CHUNKS[k]
        pixels = source.reshape(height, width * stacked, lanes)
        return pltpu.make_async_copy(
            pixels.at[first:last, :, lanes_of(tile)], xbuf.at[place, first:last], x_sems.at[place, k]
        )

    def start_x(at):
        @pl.when(at < targets)
        def _():
            for k in range(len(ROW_CHUNKS)):
                x_copy(y_any, jnp.minimum(at, targets - 1) + section, at, k).start()

        @pl.when((at >= targets) & (at < steps))
        def _():
            for k in range(len(ROW_CHUNKS)):
                x_copy(x_any, jnp.clip(at - targets, 0, tiles - 1), at, k).start()

    tile = jnp.maximum(step - targets, 0)
    outs = ((a1, a1_any), (s1, s1_any), (a2, a2_any), (s2, s2_any), (s3, s3_any), (fb, f_any))

    def out_copy(k, at):
        source, into = outs[k]
        place = into.at[:, lanes_of(at)] if k == 5 else into.at[at]
        return pltpu.make_async_copy(source, place, out_sems.at[k])

    def wait_outs(which):
        @pl.when(step > targets)
        def _():
            for k in which:
                out_copy(k, jnp.maximum(tile - 1, 0)).wait()

    def start_outs(which):
        @pl.when(online)
        def _():
            for k in which:
                out_copy(k, tile).start()

    def swap():
        return pltpu.make_async_remote_copy(
            src_ref=late.at[:, lanes_of((tiles - 1) * section)],
            dst_ref=late.at[:, lanes_of((tiles - 1) * section)],
            send_sem=sent,
            recv_sem=came,
            device_id=(1 - section, batch),
            device_id_type=MESH,
        )

    def dense_copy(source):
        return pltpu.make_async_copy(source, wd, wd_sem)

    @pl.when(step == 0)
    def _():
        barrier = pltpu.get_barrier_semaphore()
        pl.semaphore_signal(barrier, inc=1, device_id=(1 - section, batch), device_id_type=MESH)
        start_x(step)
        dense_copy(target_dense_any).start()

    start_x(step + 1)

    def prepare(one_ref, two_ref, three_ref, off_one, off_two, off_three):
        wt1[...] = jnp.zeros_like(wt1)
        wt2[...] = jnp.zeros_like(wt2)
        wt3[...] = jnp.zeros_like(wt3)
        base = nt_dot(eye(32), nn_dot(p1_ref[...], one_ref[...]).astype(BF16))
        base = (0.5 * base).astype(BF16)
        for t in range(5):
            for u in range(8):
                wt1[32 * t : 32 * t + 32, 96 * u + 16 * t : 96 * u + 16 * t + 32] = base[:, 32 * u : 32 * u + 32]
        base = nt_dot(eye(64), nn_dot(p2_ref[...], two_ref[...]).astype(BF16))
        base = (0.5 * base).astype(BF16)
        for t in range(3):
            for u in range(4):
                wt2[64 * t : 64 * t + 64, 256 * u + 64 * t : 256 * u + 64 * t + 128] = base[:, 128 * u : 128 * u + 128]
        for u in range(3):
            for v in range(3):
                piece = (0.5 * three_ref[3 * u + v].astype(F32)).astype(BF16)
                wt4[:, 192 * u + 64 * v : 192 * u + 64 * v + 64] = piece
                for t in range(2):
                    at = 256 * u + 64 * t + 64 * v
                    wt3[64 * t : 64 * t + 64, at : at + 64] = piece
        c1[...] = stack([0.5 * lane_bias(off_one[...], 32)] * 5)
        c2[...] = stack([0.5 * lane_bias(off_two[...], 64)] * 3)
        column = 0.5 * lane_bias(off_three[...], 64)
        c3[...] = stack([column] * 2)
        c4[...] = column

    @pl.when(step == 0)
    def _():
        prepare(v1_ref, v2_ref, v3_ref, q1_ref, q2_ref, q3_ref)

    @pl.when(step == targets)
    def _():
        prepare(w1_ref, w2_ref, w3_ref, o1_ref, o2_ref, o3_ref)

    def put(bias, act, slope, places):
        def then(value):
            for k, (row, at, size) in enumerate(places):
                a, s = activate(value[:, LANES * k : LANES * k + LANES] + bias[...])
                act[row, at : at + size, :] = a.astype(BF16)
                slope[row, at : at + size, :] = s.astype(BF16)

        return then

    def strips_one(i, s):
        def dot():
            cols = [
                stack([xbuf[slot, 8 * i + 4 * k + u, 80 * s : 80 * s + 96, :] for u in range(8)])
                for k in range(2)
            ]
            return nn_dot(wt1[...], beside(cols))

        return dot, put(c1, a1, s1, [(2 * i + k, 160 * s, 160) for k in range(2)])

    wait_outs((0, 1))
    for k, pairs in enumerate((range(0, 4), range(4, 10))):
        x_copy(x_any, tile, step, k).wait()
        in_turn([strips_one(i, s) for i in pairs for s in range(4)])
    start_outs((0, 1))
    wait_outs((2, 3, 4, 5))

    def strips_two(places):
        def dot():
            cols = [
                stack([a1[2 * p + u, 192 * s : 192 * s + 256, :] for u in range(4)])
                for p, s in places
            ]
            return nn_dot(wt2[...], beside(cols))

        return dot, put(c2, a2, s2, [(p, 192 * s, 192) for p, s in places])

    def strips_three(places, weight, bias, count):
        def dot():
            cols = [
                stack([a2[p + u, 64 * q : 64 * q + 64 * count + 128, :] for u in range(3)])
                for p, q in places
            ]
            return nn_dot(weight[...], beside(cols))

        def then(value):
            for k, (p, q) in enumerate(places):
                a, s = activate(value[:, LANES * k : LANES * k + LANES] + bias[...])
                for t in range(count):
                    fs[pl.ds(7 * p + q + t, 64, stride=49), :] = a[64 * t : 64 * t + 64, :]
                s3[p, 64 * q : 64 * q + 64 * count, :] = s.astype(BF16)

        return dot, then

    two = [(2 * i + k, s) for i in range(4) for s in range(3) for k in range(2)]
    two += [(8, s) for s in range(3)]
    three = [(p, q) for p in range(7) for q in (0, 2, 4)]
    ends = [(p, 6) for p in range(7)]
    in_turn(
        [strips_two(two[k : k + 2]) for k in range(0, len(two), 2)]
        + [strips_three(three[k : k + 2], wt3, c3, 2) for k in range(0, len(three), 2)]
        + [strips_three(ends[k : k + 2], wt4, c4, 1) for k in range(0, len(ends), 2)]
    )
    fb[...] = fs[...].astype(BF16)
    start_outs((2, 3, 4, 5))

    def turn(source):
        dense_copy(source).wait()
        unit = eye(512)
        for at in range(0, wd.shape[0], 256):
            size = min(256, wd.shape[0] - at)
            wdt[:, at : at + size] = nt_dot(unit, wd[at : at + size, :]).astype(BF16)

    @pl.when(step == 0)
    def _():
        turn(target_dense_any)
        dense_copy(dense_any).start()

    @pl.when(step == targets)
    def _():
        turn(dense_any)

    def column(rows_ref):
        return stack([lane_bias(rows_ref[k : k + 1, :], LANES) for k in range(rows_ref.shape[0])])

    pre[...] = nn_dot(wdt[...], fb[...])

    @pl.when(step < targets)
    def _():
        later, _ = activate(0.5 * (pre[...] + column(d1_ref)))
        late[:, lanes_of(jnp.minimum(step, targets - 1) + section)] = later.astype(BF16)

    @pl.when(step == targets - 1)
    def _():
        pl.semaphore_wait(pltpu.get_barrier_semaphore(), 1)
        swap().start()

    @pl.when(online)
    def _():
        hidden[:, lanes_of(tile)] = pre[...] + column(b1_ref)

    @pl.when(step == steps - 1)
    def _():
        count = out_ref.shape[0]
        back[...] = jnp.zeros_like(back)
        lgs[...] = jnp.zeros_like(lgs)
        for at in range(0, count, 256):
            size = min(256, count - at)
            back[:, at : at + size] = nt_dot(eye(512), out_ref[at : at + size, :]).astype(BF16)

        def wide(ref):
            return beside([lane_column(ref[...].reshape(1, count))] * tiles)

        active, slope = activate(0.5 * hidden[...])
        active = active.astype(BF16)
        active_ref[...] = active
        logits[...] = nn_dot(out_ref[...], active) + wide(b2_ref)
        swap().wait()
        logits_later[...] = nn_dot(target_out_ref[...], late[...]) + wide(d2_ref)

        def row(ref):
            return beside([ref[k : k + 1, :] for k in range(tiles)])

        action, later_action = row(action_ref), row(later_action_ref)
        length, terminal = row(length_ref), row(terminal_ref)

        def pick(ref, ids):
            total = jnp.zeros((ATOMS, lanes), F32)
            for a in range(ACTIONS):
                total = total + jnp.where(ids == a, ref[ATOMS * a : ATOMS * a + ATOMS, :], 0.0)
            return total

        soft, log_soft = softmax_terms(pick(logits, action))
        returns = jnp.zeros((1, lanes), F32)
        bootstrap = jnp.zeros((1, lanes), F32)
        product = jnp.ones((1, lanes), F32)
        for k in range(NSTEP):
            returns = returns + jnp.where(length > k, product * rewards_ref[k : k + 1, :], 0.0)
            product = product * discounts_ref[k : k + 1, :]
            bootstrap = bootstrap + jnp.where(length == k + 1, product, 0.0)
        bootstrap = bootstrap * (1.0 - terminal.astype(F32))
        spacing = (support_high - support_low) / (ATOMS - 1)
        ids = lax.broadcasted_iota(jnp.int32, (ATOMS, lanes), 0).astype(F32)
        shifted = jnp.clip(returns + bootstrap * (support_low + spacing * ids), support_low, support_high)
        position[...] = (shifted - support_low) / spacing
        probs[...], _ = softmax_terms(pick(logits_later, later_action))
        mass = jnp.zeros((ATOMS, lanes), F32)
        for j in range(ATOMS):
            weight = jnp.maximum(0.0, 1.0 - jnp.abs(position[j : j + 1, :] - ids))
            mass = mass + probs[j : j + 1, :] * weight
        loss_ref[...] = -jnp.sum(mass * log_soft, axis=0, keepdims=True)
        chosen_grad = jnp.sum(mass, axis=0, keepdims=True) * soft - mass
        for a in range(ACTIONS):
            lgs[ATOMS * a : ATOMS * a + ATOMS, :] = jnp.where(action == a, chosen_grad, 0.0)
        lg = lgs[...].astype(BF16)
        lg_ref[...] = lg[0:count]
        hg = (nn_dot(back[...], lg) * (0.5 * slope)).astype(BF16)
        hg_ref[...] = hg
        ones = jnp.ones((8, lanes), BF16)
        sum1_ref[...] = nt_dot(ones, hg)
        sum2_ref[...] = nt_dot(ones, lg[0:count])
        for k in range(len(outs)):
            out_copy(k, tile).wait()


def head(x, y, dense_one, target_dense_one, small):
    lanes = x.shape[3]
    count = small[14].shape[0]
    tiles = lanes // LANES
    outs = [(20, 640), (20, 640), (9, 576), (9, 576), (7, 448)]
    outs = [(tiles,) + shape + (LANES,) for shape in outs] + [(3136, lanes)]
    rest = [((512, lanes), BF16), ((count, lanes), BF16), ((512, lanes), BF16), ((1, lanes), F32)]
    rest += [((8, 512), F32), ((8, count), F32)]
    anywhere = pl.BlockSpec(memory_space=pl.ANY)
    buffers = [
        ((160, 768), BF16),
        ((192, 1024), BF16),
        ((128, 768), BF16),
        ((64, 576), BF16),
        ((160, LANES), F32),
        ((192, LANES), F32),
        ((128, LANES), F32),
        ((64, LANES), F32),
        ((3136, LANES), F32),
        ((3136, LANES), BF16),
        ((2, 84, 336, LANES), BF16),
        ((20, 640, LANES), BF16),
        ((20, 640, LANES), BF16),
        ((9, 576, LANES), BF16),
        ((9, 576, LANES), BF16),
        ((7, 448, LANES), BF16),
        ((3136, 512), BF16),
        ((512, 3136), BF16),
        ((512, LANES), F32),
        ((512, lanes), F32),
        ((512, lanes), BF16),
        ((512, 1024), BF16),
        ((count, lanes), F32),
        ((count, lanes), F32),
        ((1024, lanes), F32),
        ((ATOMS, lanes), F32),
        ((ATOMS, lanes), F32),
    ]
    return pl.pallas_call(
        head_kernel,
        grid=(2 * (lanes // LANES) - 1,),
        in_specs=[anywhere] * 4 + [whole(a.shape) for a in small],
        out_specs=[anywhere] * len(outs) + [whole(s) for s, _ in rest],
        out_shape=[jax.ShapeDtypeStruct(s, BF16) for s in outs]
        + [jax.ShapeDtypeStruct(s, t) for s, t in rest],
        scratch_shapes=[pltpu.VMEM(s, t) for s, t in buffers]
        + [
            pltpu.SemaphoreType.DMA((2, len(ROW_CHUNKS))),
            pltpu.SemaphoreType.DMA((len(outs),)),
            pltpu.SemaphoreType.DMA,
            pltpu.SemaphoreType.DMA,
            pltpu.SemaphoreType.DMA,
        ],
        compiler_params=pltpu.CompilerParams(
            collective_id=0, has_side_effects=True, vmem_limit_bytes=60 * 1024 * 1024
        ),
        cost_estimate=pl.CostEstimate(
            flops=5 * 2 * 9785600 * LANES, bytes_accessed=2**26, transcendentals=0
        ),
    )(x, y, dense_one, target_dense_one, *small)


def backward_kernel(
    capacity,
    a2_ref,
    s2_ref,
    s3_ref,
    a1_any,
    s1_any,
    x_any,
    f_any,
    dense_weight_any,
    hg_ref,
    lg_ref,
    active_ref,
    w1_ref,
    w2_ref,
    w3_ref,
    p2_ref,
    q1_ref,
    owner_ref,
    loss_ref,
    sum1_ref,
    sum2_ref,
    frames_any,
    dense_any,
    sum_ref,
    own_ref,
    t1_ref,
    t2_ref,
    t3_ref,
    tb_ref,
    fcs,
    stage,
    turned,
    first,
    packed,
    wb2,
    wb3,
    g2,
    g3,
    g1,
    frames,
    wb1,
    frame_sems,
    dense_sem,
    a1_ref,
    s1_ref,
    xbuf,
    fbuf,
    dense_weight_ref,
    weight_sem,
    slab,
    landed,
    shared,
    a_sems,
    x_sem,
    f_sem,
    sent,
    came,
    pack,
    arrived,
    total,
    crossed,
    share,
    gathered,
    left,
    reached,
):
    section, batch = lax.axis_index("section"), lax.axis_index("batch")
    owners = lax.axis_size("batch")
    bits = owners.bit_length() - 1
    tile = pl.program_id(0)
    last_tile = pl.num_programs(0) - 1

    dense_rows = slab.shape[0]
    bit = [lax.rem(batch // (1 << k), 2) for k in range(bits)]
    colours = 2 if bits < 7 else 1
    region = dense_rows // (2 * colours)
    orders = [list(range(1, bits)) for _ in range(colours)]
    orders[-1] = orders[-1][(bits - 1) // 2 :] + orders[-1][: (bits - 1) // 2]
    base = (dense_rows // 2) * bit[0]
    bases = []
    for c in range(colours):
        starts = [base + c * region]
        for m, k in enumerate(orders[c]):
            starts.append(starts[-1] + (region >> (m + 1)) * bit[k])
        bases.append(starts)

    def rows_at(start, size):
        return pl.ds(pl.multiple_of(start, 16), size)

    def moves(phase):
        if phase in (0, 2 * bits - 1):
            half = dense_rows // 2
            if phase:
                return [(0, base, half, None, None)]
            return [(0, half * (1 - bit[0]), half, 0, base)]
        found = []
        for c in range(colours):
            m = phase - 1 if phase < bits else 2 * bits - 2 - phase
            size = region >> (m + 1)
            k, start = orders[c][m], bases[c][m]
            if phase < bits:
                place = dense_rows // 2 + (c + 1) * region - 2 * size
                found.append((k, start + size * (1 - bit[k]), size, place, bases[c][m + 1]))
            else:
                found.append((k, bases[c][m + 1], size, None, None))
        return found

    def transfers(phase):
        copies = []
        for c, (k, start, size, place, _) in enumerate(moves(phase)):
            if phase < bits:
                source, into = slab.at[rows_at(start, size), :], landed.at[pl.ds(place, size), :]
            else:
                source = into = shared.at[rows_at(start, size), :]
            copies.append(
                pltpu.make_async_remote_copy(
                    src_ref=source,
                    dst_ref=into,
                    send_sem=sent.at[2 * phase + c],
                    recv_sem=came.at[2 * phase + c],
                    device_id=(section, batch + (1 << k) * (1 - 2 * bit[k])),
                    device_id_type=MESH,
                )
            )
        return copies

    def complete(phase):
        for copy, (_, _, size, place, to) in zip(transfers(phase), moves(phase)):
            copy.wait()
            if phase < bits:
                step = min(size, 64)

                def add(n, carry, step=step, place=place, to=to):
                    at = rows_at(to + step * n, step)
                    more = landed[pl.ds(pl.multiple_of(place + step * n, 16), step), :]
                    slab[at, :] = (slab[at, :].astype(F32) + more.astype(F32)).astype(BF16)
                    return carry

                lax.fori_loop(0, size // step, add, 0)
        if phase == bits - 1:
            for c in range(colours):
                own = rows_at(bases[c][-1], region >> (bits - 1))
                shared[own, :] = slab[own, :]

    starts = [0, 1, 2, 3, 5, 6, 8]
    if bits != 4:
        starts = [9 * phase // (2 * bits - 1) for phase in range(2 * bits - 1)]
    last_phase = 2 * bits - 1

    def slot(index):
        for phase, at in enumerate(starts):
            if phase > 0 and at % 3 == index:

                @pl.when(tile == at // 3)
                def _(phase=phase):
                    complete(phase - 1)
                    for copy in transfers(phase):
                        copy.start()

    high_count = owners // 4
    block = high_count * SLICE
    low, high = lax.rem(batch, 4), batch // 4
    group = section * 4 + low
    place = low * high_count + high

    def near(k):
        index = lax.rem(group + k, 8)
        return index, (index // 4, high * 4 + lax.rem(index, 4))

    def far(k):
        index = lax.rem(high + k, high_count)
        return index, (section, index * 4 + low)

    def send(source, into, device, number):
        return pltpu.make_async_remote_copy(
            src_ref=source,
            dst_ref=into,
            send_sem=left.at[number],
            recv_sem=reached.at[number],
            device_id=device,
            device_id_type=MESH,
        )

    def rows_of(index, size):
        return pl.ds(pl.multiple_of(index * size, size), size)

    def to_near(k):
        index, device = near(k)
        return send(pack.at[rows_of(index, block), :], arrived.at[group], device, k)

    short = high_count <= 4

    def to_far(k):
        index, device = far(k)
        source = crossed.at[high] if short else total.at[rows_of(index, SLICE), :]
        return send(source, crossed.at[high], device, 8 + k)

    def back_far(k):
        return send(share, gathered.at[place], far(k)[1], 8 + high_count + k)

    def back_near(k):
        ours = gathered.at[pl.ds(low * high_count, high_count)]
        device = (section, high * 4 + lax.rem(low + k, 4))
        return send(ours, ours, device, 8 + 2 * high_count + k)

    def a_copy(at, k):
        source, into = ((a1_any, a1_ref), (s1_any, s1_ref))[k]
        return pltpu.make_async_copy(source.at[at], into, a_sems.at[k])

    def dense_copy():
        return pltpu.make_async_copy(shared, dense_any, dense_sem)

    height, width, stacked, lane_count = x_any.shape
    pixels = x_any.reshape(height, width * stacked, lane_count)

    def x_copy():
        return pltpu.make_async_copy(
            pixels.at[pl.ds(40 * section, 44), :, pl.ds(pl.multiple_of(tile * LANES, LANES), LANES)],
            xbuf,
            x_sem,
        )

    def f_copy():
        half = fbuf.shape[0]
        return pltpu.make_async_copy(f_any.at[rows_at(half * section, half), :], fbuf, f_sem)

    def weight_copy():
        return pltpu.make_async_copy(dense_weight_any, dense_weight_ref, weight_sem)

    @pl.when(tile == 0)
    def _():
        f_copy().start()
        weight_copy().start()
        for k in range(2):
            a_copy(tile, k).start()
        barrier = pltpu.get_barrier_semaphore()
        for k in range(1, 8):
            pl.semaphore_signal(barrier, inc=1, device_id=near(k)[1], device_id_type=MESH)
        for k in range(1, high_count):
            pl.semaphore_signal(barrier, inc=1, device_id=far(k)[1], device_id_type=MESH)
        f_copy().wait()

        def dense_one(start, stop):
            for at in range(start, stop, 256):
                rows = slice(at, min(at + 256, stop))
                slab[rows, :] = nt_dot(fbuf[rows, :], hg_ref[...]).astype(BF16)

        def upper_half():
            slab[1568:dense_rows, :] = jnp.zeros((dense_rows - 1568, 512), BF16)
            mine = active_ref[pl.ds(pl.multiple_of(256 * section, 256), 256), :]
            slab[1568:2032, 0:256] = nt_dot(lg_ref[0:464, :], mine).astype(BF16)
            slab[1568:2022, 256:512] = nt_dot(lg_ref[464:918, :], mine).astype(BF16)
            dense_one(1024, 1568)

        @pl.when(bit[0] == 0)
        def _():
            upper_half()

        @pl.when(bit[0] == 1)
        def _():
            dense_one(0, 1024)

        pl.semaphore_wait(barrier, 6 + high_count)
        for copy in transfers(0):
            copy.start()

        @pl.when(bit[0] == 0)
        def _():
            dense_one(0, 1024)

        @pl.when(bit[0] == 1)
        def _():
            upper_half()

        for ref in (t1_ref, t2_ref, t3_ref, tb_ref, wb1, wb2, wb3):
            ref[...] = jnp.zeros_like(ref)
        for ref, edge, width in ((g1, 1, 32), (g2, 1, 64), (g3, 2, 64)):
            side = jnp.zeros((edge * width, LANES), BF16)
            for r in range(ref.shape[0]):
                if edge <= r < ref.shape[0] - edge:
                    ref[r, 0 : edge * width, :] = side
                    ref[r, ref.shape[1] - edge * width :, :] = side
                else:
                    ref[r] = jnp.zeros((ref.shape[1], LANES), BF16)
        rows = (0.5 * nn_dot(p2_ref[...], w2_ref[...])).astype(BF16)
        for dp in range(2):
            for dq in range(2):
                for b in range(2):
                    for x in range(2):
                        u, v = b + 2 * (1 - dp), x + 2 * (1 - dq)
                        to, at, of = 32 * (2 * b + x), 64 * (2 * dp + dq), 32 * (4 * u + v)
                        wb2[to : to + 32, at : at + 64] = rows[of : of + 32, :]
        for u in range(3):
            for v in range(3):
                piece = (0.5 * nt_dot(eye(64), w3_ref[3 * u + v])).astype(BF16)
                for t in range(3):
                    at = 320 * (2 - u) + 64 * (t + 2 - v)
                    wb3[64 * t : 64 * t + 64, at : at + 64] = piece
        half = w1_ref[pl.ds(pl.multiple_of(section * 128, 128), 128), :]
        pieces = nn_dot(q1_ref[...], half).astype(BF16)
        for k in range(16):
            wb1[:, 32 * k : 32 * k + 32] = pieces[224 * k : 224 * k + 224, :]
        weight_copy().wait()

    slot(0)
    x_copy().start()

    def sums(value, size):
        total = value[0:size]
        for at in range(size, value.shape[0], size):
            total = total + value[at : at + size]
        return total

    hg = hg_ref[:, pl.ds(pl.multiple_of(tile * LANES, LANES), LANES)]

    def feature_grad(n, carry):
        at = pl.ds(pl.multiple_of(448 * n, 448), 448)
        fcs[at, :] = 0.5 * nn_dot(dense_weight_ref[at, :], hg).astype(BF16).astype(F32)
        return carry

    lax.fori_loop(0, 7, feature_grad, 0, unroll=True)

    def cot_three(p, carry):
        cot = stack([fcs[pl.ds(7 * p + q, 64, stride=49), :] for q in range(7)])
        g = cot * s3_ref[p].astype(F32)
        g3[p + 2, 128:576, :] = g.astype(BF16)
        tb_ref[96:160, :] += sums(g, 64)
        return carry

    lax.fori_loop(0, 7, cot_three, 0, unroll=True)

    blocks, cots = [], []
    nothing = jnp.zeros((64, LANES), BF16)
    for n in range(4):
        p = 4 * section + n
        rows = [jnp.minimum(p + u, 8) for u in range(3)]
        blocks.append(stack([a2_ref[r, 0:384, :] for r in rows]))
        blocks.append(stack([part for r in rows for part in (a2_ref[r, 256:576, :], nothing)]))
        cots += [g3[p + 2, 128:384, :], g3[p + 2, 384:640, :]]
    t3_ref[...] += nt_dot(beside(blocks), beside(cots))


    def patch_three(y, s):
        return stack([g3[y + d, 192 * s : 192 * s + 320, :] for d in range(3)])

    def strips_two(places):
        def dot():
            return nn_dot(wb3[...], beside([patch_three(y, s) for y, s in places]))

        def then(value):
            for k, (y, s) in enumerate(places):
                slope = s2_ref[y, 192 * s : 192 * s + 192, :].astype(F32)
                g = value[:, LANES * k : LANES * k + LANES] * slope
                g2[y + 1, 64 + 192 * s : 256 + 192 * s, :] = g.astype(BF16)
                tb_ref[32:96, :] += sums(g, 64)

        return dot, then

    pairs = [(2 * i, s) for i in range(4) for s in range(3)]
    in_turn(
        [strips_two([(y, s), (y + 1, s)]) for y, s in pairs]
        + [strips_two([(8, 0), (8, 1)]), strips_two([(8, 2)])]
    )

    slot(1)
    a_copy(tile, 0).wait()
    a_copy(tile, 1).wait()

    blocks, cots = [], []
    for n in range(5):
        p = 5 * section + n
        rows = [jnp.minimum(2 * p + u, 19) for u in range(4)]
        for q in range(3):
            blocks.append(stack([a1_ref[r, 192 * q : 192 * q + 256, :] for r in rows]))
            cots.append(g2[p + 1, 64 + 192 * q : 256 + 192 * q, :])
    t2_ref[...] += nt_dot(beside(blocks), beside(cots))


    def back_two(i):
        def strip(s):
            def dot():
                cols = [
                    stack([g2[2 * i + k + d, 64 * s : 64 * s + 128, :] for d in range(2)])
                    for k in range(2)
                ]
                return nn_dot(wb2[...], beside(cols))

            def then(v):
                total = jnp.zeros((32, LANES), F32)
                for k in range(2):
                    for b in range(2):
                        row = 4 * i + 2 * k + b
                        slope = s1_ref[row, 64 * s : 64 * s + 64, :].astype(F32)
                        g = v[64 * b : 64 * b + 64, LANES * k : LANES * k + LANES] * slope
                        g1[row + 1, 32 + 64 * s : 96 + 64 * s, :] = g.astype(BF16)
                        total = total + sums(g, 32)
                tb_ref[0:32, :] += total

            return dot, then

        return [strip(s) for s in range(10)]

    in_turn([job for i in range(5) for job in back_two(i)])
    slot(2)

    @pl.when(tile < last_tile)
    def _():
        for k in range(2):
            a_copy(tile + 1, k).start()

    x_copy().wait()

    for first_row in (0, 5):
        blocks, cots = [], []
        for n in range(first_row, first_row + 5):
            for q in range(4):
                blocks.append(stack([xbuf[4 * n + u, 80 * q : 80 * q + 96, :] for u in range(8)]))
                cots.append(g1[10 * section + n + 1, 32 + 160 * q : 192 + 160 * q, :])
        t1_ref[...] += nt_dot(beside(blocks), beside(cots))


    height, width, channels, lane_count = frames_any.shape
    out_pixels = frames_any.reshape(height, width * channels, lane_count)

    def frames_copy(at, part):
        lanes = pl.ds(pl.multiple_of(at * LANES, LANES), LANES)
        rows = pl.ds(28 * part, 28)
        return pltpu.make_async_copy(frames.at[rows], out_pixels.at[rows, :, lanes], frame_sems.at[part])

    def frames_part(part):
        def strips(places):
            def dot():
                cols = [
                    stack([g1[7 * part + a + d, 224 * s : 224 * s + 256, :] for d in range(2)])
                    for a, s in places
                ]
                return nn_dot(wb1[...], beside(cols))

            def then(v):
                for k, (a, s) in enumerate(places):
                    for i in range(4):
                        frames[28 * part + 4 * a + i, 56 * s : 56 * s + 56, :] = v[
                            56 * i : 56 * i + 56, LANES * k : LANES * k + LANES
                        ].astype(BF16)

            return dot, then

        places = [(a, s) for a in range(7) for s in range(3)]
        in_turn([strips(places[k : k + 2]) for k in range(0, len(places), 2)])

    @pl.when(tile < last_tile)
    def _():
        def one_part(part, carry):
            @pl.when(tile > 0)
            def _():
                frames_copy(tile - 1, part).wait()

            frames_part(part)
            frames_copy(tile, part).start()
            return carry

        lax.fori_loop(0, 3, one_part, 0)

    def last_part(part):
        frames_copy(tile - 1, part).wait()
        frames_part(part)
        frames_copy(tile, part).start()

    @pl.when(tile == last_tile)
    def _():
        rows = owner_ref.shape[1]
        half_rows = SLICE * owners
        owner_hot = owner_ref[...] == lax.broadcasted_iota(jnp.int32, (owners, rows), 0)
        owner_hot = jnp.where(owner_hot, 1.0, 0.0)
        before = lax.broadcasted_iota(jnp.int32, (rows, rows), 0)
        before = before < lax.broadcasted_iota(jnp.int32, (rows, rows), 1)
        before = nn_dot(owner_hot.astype(BF16), jnp.where(before, 1.0, 0.0).astype(BF16))
        slots = jnp.sum(before * owner_hot, axis=0, keepdims=True)
        slot_ids = lax.broadcasted_iota(jnp.int32, (32, rows), 0)
        slot_ids = slot_ids - capacity * (batch // SLICE)
        slot_hot = jnp.where(slots.astype(jnp.int32) == slot_ids, 1.0, 0.0).astype(BF16)
        outgoing = nt_dot((owner_hot * loss_ref[...]).astype(BF16), slot_hot)
        count = sum2_ref.shape[1] // 2
        for k in range(9):
            u, v = k // 3, k % 3
            pieces = [
                t3_ref[384 * u + 64 * (q + v) : 384 * u + 64 * (q + v) + 64, 64 * q : 64 * q + 64]
                for q in range(4)
            ]
            turned[64 * k : 64 * k + 64, 0:64] = functools.reduce(jnp.add, pieces)
        for k in range(16):
            u, v = k // 4, k % 4
            pieces = [
                t2_ref[256 * u + 32 * (2 * q + v) : 256 * u + 32 * (2 * q + v) + 32, 64 * q : 64 * q + 64]
                for q in range(3)
            ]
            turned[32 * k : 32 * k + 32, 64:128] = functools.reduce(jnp.add, pieces)
        for u in range(8):
            pieces = [
                t1_ref[96 * u + 16 * q : 96 * u + 16 * q + 32, 32 * q : 32 * q + 32] for q in range(5)
            ]
            first[32 * u : 32 * u + 32, 0:32] = functools.reduce(jnp.add, pieces)
        both = jnp.transpose(turned[...])
        ones = jnp.ones((8, LANES), F32)
        bias = lax.dot_general(
            ones, tb_ref[...], NT, precision=lax.Precision.HIGHEST, preferred_element_type=F32
        )
        for h in range(2):
            packed[...] = jnp.zeros_like(packed)
            for k in range(9):
                packed[32 * k : 32 * k + 32, 0:64] = both[32 * h : 32 * h + 32, 64 * k : 64 * k + 64]
            for k in range(16):
                piece = both[64 + 32 * h : 96 + 32 * h, 32 * k : 32 * k + 32]
                stage[pl.ds(k, 32, stride=16), :] = jnp.pad(piece, ((0, 0), (0, 96)))
            packed[0:512, 64:96] = stage[:, 0:32]
            for c in range(4):
                rows_c = first[pl.ds(c, 64, stride=4), :]
                packed[288 : 352, 16 * c : 16 * c + 16] = rows_c[:, 16 * h : 16 * h + 16]
            packed[352 : 353, 0:16] = bias[0:1, 16 * h : 16 * h + 16]
            packed[353 : 354, 0:32] = bias[0:1, 32 + 32 * h : 64 + 32 * h]
            packed[354 : 355, 0:32] = bias[0:1, 96 + 32 * h : 128 + 32 * h]
            packed[355 : 356, 0:1] = jnp.sum(loss_ref[...], axis=1, keepdims=True)
            for k in range(4):
                packed[384 + k : 385 + k, 0:64] = sum1_ref[0:1, 256 * h + 64 * k : 256 * h + 64 * k + 64]
            for k in range(8):
                at = 64 * k
                size = min(64, count - at)
                packed[388 + k : 389 + k, 0:size] = sum2_ref[0:1, count * h + at : count * h + at + size]
            for o in range(owners):
                at = SLICE * ((o % 4) * (owners // 4) + o // 4)
                packed[pl.ds(at + lax.rem(batch, SLICE), 1), 96:128] = outgoing[o : o + 1, :]
            pack[half_rows * h : half_rows * h + half_rows, :] = packed[...].astype(BF16)
        for k in range(1, 8):
            to_near(k).start()
        last_part(0)
        total[...] = pack[rows_of(group, block), :].astype(F32)
        for k in range(1, 8):
            to_near(k).wait()
            total[...] += arrived[lax.rem(group + 8 - k, 8)].astype(F32)
        if short:
            crossed[high] = total[...].astype(BF16)
            for k in range(1, high_count):
                to_far(k).start()
            last_part(1)
            complete(last_phase - 1)
            for copy in transfers(last_phase):
                copy.start()
            for k in range(1, high_count):
                to_far(k).wait()
            ours = crossed[0].astype(F32)
            for k in range(1, high_count):
                ours = ours + crossed[k].astype(F32)
            total[...] = ours
            for k in range(high_count):
                gathered[low * high_count + k] = ours[SLICE * k : SLICE * k + SLICE, :]
            own_ref[...] = total[rows_of(high, SLICE), :]
        else:
            for k in range(1, high_count):
                to_far(k).start()
            last_part(1)
            complete(last_phase - 1)
            for copy in transfers(last_phase):
                copy.start()
            share[...] = total[rows_of(high, SLICE), :]
            for k in range(1, high_count):
                to_far(k).wait()
                share[...] += crossed[lax.rem(high + high_count - k, high_count)]
            for k in range(1, high_count):
                back_far(k).start()
            gathered[place] = share[...]
            own_ref[...] = share[...]
            for k in range(1, high_count):
                back_far(k).wait()
        for k in range(1, 4):
            back_near(k).start()
        last_part(2)
        complete(last_phase)
        dense_copy().start()
        for k in range(1, 4):
            back_near(k).wait()
        sum_ref[...] = gathered[0:16]
        dense_copy().wait()
        for part in range(3):
            frames_copy(tile, part).wait()


def backward(tiles, anys, hg, lg, active, w1, w2, w3, p2, q1, owners, owner_count, capacity, losses, sum1, sum2):
    lanes = hg.shape[-1]
    small = (hg, lg, active, w1, w2, w3, p2, q1, owners, losses, sum1, sum2)
    totals = [(768, 160), (1024, 192), (1152, 256), (160, LANES), (3136, LANES), (512, LANES)]
    totals += [(576, LANES), (256, LANES)]
    pack_shape = (2 * SLICE * owner_count, LANES)
    dense_shape = (2048, 512)
    frames_shape = (84, 84, 2, lanes)
    high_count = owner_count // 4
    copies = 8 + 2 * high_count + 4
    transfers = 4 * (owner_count.bit_length() - 1)
    return pl.pallas_call(
        functools.partial(backward_kernel, capacity),
        grid=(lanes // LANES,),
        in_specs=[pl.BlockSpec((None,) + a.shape[1:], lambda i: (i, 0, 0, 0)) for a in tiles]
        + [pl.BlockSpec(memory_space=pl.ANY)] * len(anys)
        + [whole(a.shape) for a in small],
        out_specs=[pl.BlockSpec(memory_space=pl.ANY)] * 2 + [whole((16, SLICE, LANES)), whole((SLICE, LANES))],
        out_shape=[jax.ShapeDtypeStruct(s, BF16) for s in (frames_shape, dense_shape)]
        + [jax.ShapeDtypeStruct(s, F32) for s in ((16, SLICE, LANES), (SLICE, LANES))],
        scratch_shapes=[pltpu.VMEM(s, F32) for s in totals + [(pack_shape[0] // 2, LANES)]]
        + [
            pltpu.VMEM((128, 256), BF16),
            pltpu.VMEM((192, 960), BF16),
            pltpu.VMEM((11, 11 * 64, LANES), BF16),
            pltpu.VMEM((11, 11 * 64, LANES), BF16),
            pltpu.VMEM((22, 704, LANES), BF16),
            pltpu.VMEM((84, 168, LANES), BF16),
            pltpu.VMEM((224, 512), BF16),
            pltpu.SemaphoreType.DMA((3,)),
            pltpu.SemaphoreType.DMA,
            pltpu.VMEM((20, 640, LANES), BF16),
            pltpu.VMEM((20, 640, LANES), BF16),
            pltpu.VMEM((44, 336, LANES), BF16),
            pltpu.VMEM((1568, lanes), BF16),
            pltpu.VMEM((3136, 512), BF16),
            pltpu.SemaphoreType.DMA,
            pltpu.VMEM(dense_shape, BF16),
            pltpu.VMEM(dense_shape, BF16),
            pltpu.VMEM(dense_shape, BF16),
            pltpu.SemaphoreType.DMA((2,)),
            pltpu.SemaphoreType.DMA,
            pltpu.SemaphoreType.DMA,
            pltpu.SemaphoreType.DMA((transfers,)),
            pltpu.SemaphoreType.DMA((transfers,)),
            pltpu.VMEM(pack_shape, BF16),
            pltpu.VMEM((8, high_count * SLICE, LANES), BF16),
            pltpu.VMEM((high_count * SLICE, LANES), F32),
            pltpu.VMEM((high_count, high_count * SLICE, LANES), BF16)
            if high_count <= 4
            else pltpu.VMEM((high_count, SLICE, LANES), F32),
            pltpu.VMEM((SLICE, LANES), F32),
            pltpu.VMEM((owner_count, SLICE, LANES), F32),
            pltpu.SemaphoreType.DMA((copies,)),
            pltpu.SemaphoreType.DMA((copies,)),
        ],
        compiler_params=pltpu.CompilerParams(
            collective_id=1, has_side_effects=True, vmem_limit_bytes=60 * 1024 * 1024
        ),
        cost_estimate=pl.CostEstimate(
            flops=3 * 7729152 * lanes, bytes_accessed=6 * 28224 * lanes, transcendentals=0
        ),
    )(*tiles, *anys, *small)


def last_kernel(
    owners,
    loss_scale,
    section_ref,
    frames_any,
    dense_ref,
    sum_ref,
    own_ref,
    out_any,
    one_ref,
    two_ref,
    k1_ref,
    k2_ref,
    k3_ref,
    o1_ref,
    o2_ref,
    o3_ref,
    d1_ref,
    d2_ref,
    loss_ref,
    table_ref,
    buffer,
    in_sems,
    out_sems,
):
    step = pl.program_id(0)
    parts = in_sems.shape[0]
    part_rows = frames_any.shape[0] // parts

    def copy_in(k):
        rows = pl.ds(part_rows * k, part_rows)
        return pltpu.make_async_copy(frames_any.at[rows], buffer.at[rows], in_sems.at[k])

    def copy_out(k):
        rows = pl.ds(part_rows * k, part_rows)
        return pltpu.make_async_copy(buffer.at[rows], out_any.at[rows], out_sems.at[k])

    @pl.when(step == 0)
    def _():
        for k in range(parts):
            copy_in(k).start()
        two_ref[0:464, :] = dense_ref[1568:2032, 0:256].astype(F32)
        two_ref[464:918, :] = dense_ref[1568:2022, 256:512].astype(F32)
        if owners == 16:
            mine = own_ref[pl.ds(pl.multiple_of(8 * section_ref[0], 8), 8), :]
            table_ref[0] = 0.5 * mine[:, 96 : 96 + table_ref.shape[2]]
        for c in range(4):
            k1_ref[64 * c : 64 * c + 64, :] = sum_ref[288:352, 16 * c : 16 * c + 16]
        k2_ref[...] = sum_ref[:, 64:96]
        k3_ref[...] = sum_ref[0:288, 0:64]
        o1_ref[...] = 0.5 * sum_ref[352:353, 0:16]
        o2_ref[...] = 0.5 * sum_ref[353:354, 0:32]
        o3_ref[...] = 0.5 * sum_ref[354:355, 0:32]
        loss_ref[...] = loss_scale * sum_ref[355:356, 0:1]
        for k in range(4):
            d1_ref[:, 64 * k : 64 * k + 64] = 0.5 * sum_ref[384 + k : 385 + k, 0:64]
        for k in range(8):
            size = min(64, 459 - 64 * k)
            d2_ref[:, 64 * k : 64 * k + size] = 0.5 * sum_ref[388 + k : 389 + k, 0:size]

        for k in range(parts):
            copy_in(k).wait()
            copy_out(k).start()

    at = pl.ds(pl.multiple_of(step * 784, 16), 784)
    one_ref[...] = dense_ref[at, :].astype(F32)

    @pl.when(step == pl.num_programs(0) - 1)
    def _():
        for k in range(parts):
            copy_out(k).wait()


def last(owners, capacity, section, frames, dense, sums, own):
    others = [(918, 256), (256, 16), (512, 32), (288, 64), (1, 16), (1, 32), (1, 32), (1, 256), (1, 459), (1, 1), (1, 8, capacity)]
    return pl.pallas_call(
        functools.partial(last_kernel, owners, 0.5 / (frames.shape[3] * owners)),
        grid=(2,),
        in_specs=[
            pl.BlockSpec(memory_space=pltpu.SMEM),
            pl.BlockSpec(memory_space=pl.ANY),
            whole(dense.shape),
            whole(sums.shape),
            whole(own.shape),
        ],
        out_specs=[pl.BlockSpec(memory_space=pl.ANY), pl.BlockSpec((784, 512), lambda i: (i, 0))]
        + [whole(a) for a in others],
        out_shape=[
            jax.ShapeDtypeStruct(frames.shape, BF16),
            jax.ShapeDtypeStruct((1568, 512), F32),
        ]
        + [jax.ShapeDtypeStruct(a, F32) for a in others],
        scratch_shapes=[
            pltpu.VMEM(frames.shape, BF16),
            pltpu.SemaphoreType.DMA((7,)),
            pltpu.SemaphoreType.DMA((7,)),
        ],
        compiler_params=pltpu.CompilerParams(vmem_limit_bytes=60 * 1024 * 1024),
        cost_estimate=pl.CostEstimate(flops=0, bytes_accessed=2**25, transcendentals=0),
    )(section, frames, dense, sums, own)


def shards(
    frames,
    next_frames,
    actions,
    next_actions,
    lengths,
    terminal,
    rewards,
    discounts,
    owners,
    conv_one_weight,
    conv_one_offset,
    conv_two_weight,
    conv_two_offset,
    conv_three_weight,
    conv_three_offset,
    dense_one_weight,
    dense_one_offset,
    dense_two_weight,
    dense_two_offset,
    target_conv_one_weight,
    target_conv_one_offset,
    target_conv_two_weight,
    target_conv_two_offset,
    target_conv_three_weight,
    target_conv_three_offset,
    target_dense_one_weight,
    target_dense_one_offset,
    target_dense_two_weight,
    target_dense_two_offset,
):
    section = lax.axis_index("section")
    owner_count = lax.axis_size("batch")
    rows = frames.shape[0]
    p1, p2, q1 = order_rows(4, 8), order_rows(32, 4), back_one_choice()

    def tower_weights(one, two, three, off_one, off_two, off_three):
        return (
            one.transpose(1, 2, 3, 0).reshape(256, 32),
            two.transpose(1, 2, 3, 0).reshape(512, 64),
            three.transpose(2, 3, 0, 1).reshape(9, 64, 64),
            off_one[None, :],
            off_two[None, :],
            off_three[None, :],
        )

    online = tower_weights(
        conv_one_weight, conv_two_weight, conv_three_weight, conv_one_offset, conv_two_offset, conv_three_offset
    )
    target = tower_weights(
        target_conv_one_weight,
        target_conv_two_weight,
        target_conv_three_weight,
        target_conv_one_offset,
        target_conv_two_offset,
        target_conv_three_offset,
    )
    x = frames.transpose(2, 3, 1, 0)
    x_next = next_frames.transpose(2, 3, 1, 0)
    section_row = section.reshape(1).astype(jnp.int32)
    vectors = [
        a.reshape(a.shape[0] // LANES, LANES)
        for a in (dense_one_offset, target_dense_one_offset, actions, next_actions, lengths, terminal)
    ]
    a1, s1, a2, s2, s3, feature, active, logit_grad, hidden_grad, row_loss, sum1, sum2 = head(
        x,
        x_next,
        dense_one_weight,
        target_dense_one_weight,
        (
            *online,
            *target,
            p1,
            p2,
            dense_two_weight.T,
            target_dense_two_weight.T,
            *vectors,
            dense_two_offset,
            target_dense_two_offset,
            rewards.T,
            discounts.T,
        ),
    )

    capacity = (rows + owner_count - 1) // owner_count + 1
    frames_grad, dense, sums, own = backward(
        (a2, s2, s3),
        (a1, s1, x, feature, dense_one_weight),
        hidden_grad,
        logit_grad,
        active,
        *online[:3],
        p2,
        q1,
        owners.T,
        owner_count,
        capacity,
        row_loss,
        sum1,
        sum2,
    )
    frames_grad, grad_dense_one, grad_dense_two, one, two, three, *rest = last(
        owner_count, capacity, section_row, frames_grad, dense, sums.reshape(16 * SLICE, LANES), own
    )
    off_one, off_two, off_three, dense_off_one, dense_off_two, loss, table = rest
    if owner_count != 16:
        groups = -(-owner_count // SLICE)
        table = 0.5 * own[:, 96 : 96 + groups * capacity].reshape(SLICE, groups, capacity)
        table = table.transpose(1, 0, 2).reshape(groups * SLICE, capacity)
        table = lax.dynamic_slice_in_dim(table, section * (owner_count // 2), owner_count // 2, 0)[None]
    return (
        loss[0, 0],
        frames_grad.transpose(3, 2, 0, 1),
        one.reshape(4, 8, 8, 16).transpose(3, 0, 1, 2),
        off_one[0],
        two.reshape(32, 4, 4, 32).transpose(0, 3, 1, 2),
        off_two[0],
        three.reshape(3, 3, 32, 64).transpose(2, 3, 0, 1),
        off_three[0],
        grad_dense_one,
        dense_off_one[0],
        grad_dense_two.T,
        dense_off_two[0],
        table,
    )


def solution(mesh):
    return jax.shard_map(
        shards,
        mesh=mesh,
        in_specs=(P("batch", None, None, None),) * 2
        + (P("batch"),) * 4
        + (P("batch", None),) * 3
        + (P(),) * 20,
        out_specs=(
            P(),
            P("batch", "section", None, None),
            P("section", None, None, None),
            P("section"),
            P("section", None, None, None),
            P("section"),
            P("section", None, None, None),
            P("section"),
            P("section", None),
            P("section"),
            P("section", None),
            P("section"),
            P("batch", "section", None),
        ),
        check_vma=False,
    )
```

time: 1420 us -> 130 us (0.09)
  matrix products: 618 us -> 0 us
  blocking collectives: 335 us -> 0 us
  local copies, waits for them, and re-layouts: 197 us -> 0 us
  Pallas kernels: 0 us -> 129 us
  waiting for transfers between devices: 105 us -> 0 us
  other arithmetic: 98.1 us -> 0 us
  starting transfers between devices: 35 us -> 0 us
  between operations: 20.6 us -> 0.83 us
    conv_general_dilated x40 -> x0, matrix products: 598 us -> none  [the longest x12 364 us: inputs_grad(): lax.conv_general_dilated(cotangent, flipped, (1, 1), ((extent, extent), (...]
    psum x2 -> x0, blocking collectives: 329 us -> none  [the longest x1 270 us: shards(): loss_sum = lax.psum(jnp.sum(all_losses), ('section', 'batch'))]
    pallas_call x0 -> x3, Pallas kernels: none -> 129 us  [the longest x1 66.5 us: backward(): pl.pallas_call(functools.partial(backward_kernel, capacity), grid=(lanes...]
    psum x1 -> x0, waiting for transfers between devices: 103 us -> none  [shards(): lax.psum((conv_totals[0], conv_totals[1], conv_totals[2], conv_totals[3],...]
    scatter x1 -> x0, local copies, waits for them, and re-layouts: 53.9 us -> none  [shards(): jnp.zeros((owner_count, capacity), jnp.float32).at[owner_ids, ranks]]
    slice x6 -> x0, local copies, waits for them, and re-layouts: 52.9 us -> none  [the longest x4 38.1 us: shards(): frames[start:stop]]
    concatenate x3 -> x0, other arithmetic: 42.8 us -> none  [the longest x1 42.6 us: shards(): all_image_grads = jnp.concatenate(image_grads, axis=0)]
    another operation x28 -> x0, local copies, waits for them, and re-layouts: 29.3 us -> none
  transfers between devices with their start and end apart: 20 -> 0, of which waited for: 2 -> 0; matrix products, arithmetic and copies ran while one was open for 51% -> 0% of each run, Pallas kernels for 0% -> 0%
where the time goes in v1:
time: 130 us
  Pallas kernels  129 us (99%)
    pallas_call x1, Pallas kernels, backward(): pl.pallas_call(functools.partial(backward_kernel, capacity), grid=(lanes...  66.5 us
    pallas_call x1, Pallas kernels, head(): pl.pallas_call(head_kernel, grid=(2 * (lanes // LANES) - 1,), in_specs=[a...  51.1 us
    pallas_call x1, Pallas kernels, last(): pl.pallas_call(functools.partial(last_kernel, owners, 0.5 / (frames.shape...  11.6 us

profile of v1, /device:TPU:1, one launch (start us, length us, event | category | flops | bytes accessed | tf_op | source)
XLA Modules:
  0.0 130.0 jit_solution(5407248421426131813)
XLA Ops:
  0.7 51.1 %shard_map.399 = (bf16[3,20,640,128]{3,2,1,0:T(8,128)(2,1)}, bf16[3,20,640,128]{3,2,1,0:T(8,128)(2,1)}, bf16[3,9,576,128]{3,2,1,0:T(8,128)(2,1)}, bf16[3,9,576,1...) custom-call(bf16[84,84,4,384]{3,2,1,0:T(4,128)(2,1)} %bitcast.56, ...), custom_call_target="tpu_custom_call" | custom-call | flops 12525568000 | bytes 67108864 | tf_op jit(solution)/shard_map/pallas_call | solution.py:500
  51.8 66.5 %shard_map.400 = (bf16[84,84,2,384]{3,2,1,0:T(2,128)(2,1)}, bf16[2048,512]{1,0:T(8,128)(2,1)}, f32[16,32,128]{2,1,0:T(8,128)}, f32[32,128]{1,0:T(8,128)}) custom-call(bf16[3,9,576,128]{3,2,1,0:T(8,128)(2,1)} %get-tuple-element.42.a2_ref, bf16[3,9,576,128]{3,2,1,0:T(8,128)(2,1)} %get-tuple-element.43.s2_ref, ...), custom_call_target="tpu_custom_call" | custom-call | flops 8903983104 | bytes 65028096 | tf_op jit(solution)/shard_map/pallas_call | solution.py:1122
  118.3 11.6 %shard_map.401 = (bf16[84,84,2,384]{3,2,1,0:T(2,128)(2,1)}, f32[1568,512]{1,0:T(8,128)}, f32[918,256]{1,0:T(8,128)}, f32[256,16]{1,0:T(8,128)}, f32[512,32]{1,0:...) custom-call(s32[1]{0:T(128)} %bitcast.section_ref, ...), custom_call_target="tpu_custom_call" | custom-call | bytes 33554432 | tf_op jit(solution)/shard_map/pallas_call | solution.py:1251

commit v2 on v1

--- a/solution.py
+++ b/solution.py
@@ -181,6 +181,12 @@
     lgs,
     probs,
     position,
+    n1,
+    n2,
+    n3,
+    m1,
+    m2,
+    m3,
     x_sems,
     out_sems,
     wd_sem,
@@ -287,13 +293,21 @@
         c3[...] = stack([column] * 2)
         c4[...] = column
 
+    now = (n1, n2, n3, m1, m2, m3)
+
     @pl.when(step == 0)
     def _():
-        prepare(v1_ref, v2_ref, v3_ref, q1_ref, q2_ref, q3_ref)
+        for to, of in zip(now, (v1_ref, v2_ref, v3_ref, q1_ref, q2_ref, q3_ref)):
+            to[...] = of[...]
 
     @pl.when(step == targets)
     def _():
-        prepare(w1_ref, w2_ref, w3_ref, o1_ref, o2_ref, o3_ref)
+        for to, of in zip(now, (w1_ref, w2_ref, w3_ref, o1_ref, o2_ref, o3_ref)):
+            to[...] = of[...]
+
+    @pl.when((step == 0) | (step == targets))
+    def _():
+        prepare(*now)
 
     def put(bias, act, slope, places):
         def then(value):
@@ -367,14 +381,13 @@
             size = min(256, wd.shape[0] - at)
             wdt[:, at : at + size] = nt_dot(unit, wd[at : at + size, :]).astype(BF16)
 
+    @pl.when((step == 0) | (step == targets))
+    def _():
+        turn(dense_any)
+
     @pl.when(step == 0)
     def _():
-        turn(target_dense_any)
         dense_copy(dense_any).start()
-
-    @pl.when(step == targets)
-    def _():
-        turn(dense_any)
 
     def column(rows_ref):
         return stack([lane_bias(rows_ref[k : k + 1, :], LANES) for k in range(rows_ref.shape[0])])
@@ -496,7 +509,7 @@
         ((1024, lanes), F32),
         ((ATOMS, lanes), F32),
         ((ATOMS, lanes), F32),
-    ]
+    ] + [(a.shape, BF16) for a in small[:6]]
     return pl.pallas_call(
         head_kernel,
         grid=(2 * (lanes // LANES) - 1,),
@@ -972,24 +985,6 @@
         places = [(a, s) for a in range(7) for s in range(3)]
         in_turn([strips(places[k : k + 2]) for k in range(0, len(places), 2)])
 
-    @pl.when(tile < last_tile)
-    def _():
-        def one_part(part, carry):
-            @pl.when(tile > 0)
-            def _():
-                frames_copy(tile - 1, part).wait()
-
-            frames_part(part)
-            frames_copy(tile, part).start()
-            return carry
-
-        lax.fori_loop(0, 3, one_part, 0)
-
-    def last_part(part):
-        frames_copy(tile - 1, part).wait()
-        frames_part(part)
-        frames_copy(tile, part).start()
-
     @pl.when(tile == last_tile)
     def _():
         rows = owner_ref.shape[1]
@@ -1056,19 +1051,22 @@
             pack[half_rows * h : half_rows * h + half_rows, :] = packed[...].astype(BF16)
         for k in range(1, 8):
             to_near(k).start()
-        last_part(0)
+
+    def after_near():
         total[...] = pack[rows_of(group, block), :].astype(F32)
         for k in range(1, 8):
             to_near(k).wait()
             total[...] += arrived[lax.rem(group + 8 - k, 8)].astype(F32)
         if short:
             crossed[high] = total[...].astype(BF16)
-            for k in range(1, high_count):
-                to_far(k).start()
-            last_part(1)
-            complete(last_phase - 1)
-            for copy in transfers(last_phase):
-                copy.start()
+        for k in range(1, high_count):
+            to_far(k).start()
+
+    def after_far():
+        complete(last_phase - 1)
+        for copy in transfers(last_phase):
+            copy.start()
+        if short:
             for k in range(1, high_count):
                 to_far(k).wait()
             ours = crossed[0].astype(F32)
@@ -1079,12 +1077,6 @@
                 gathered[low * high_count + k] = ours[SLICE * k : SLICE * k + SLICE, :]
             own_ref[...] = total[rows_of(high, SLICE), :]
         else:
-            for k in range(1, high_count):
-                to_far(k).start()
-            last_part(1)
-            complete(last_phase - 1)
-            for copy in transfers(last_phase):
-                copy.start()
             share[...] = total[rows_of(high, SLICE), :]
             for k in range(1, high_count):
                 to_far(k).wait()
@@ -1097,7 +1089,29 @@
                 back_far(k).wait()
         for k in range(1, 4):
             back_near(k).start()
-        last_part(2)
+
+    def one_part(part, carry):
+        @pl.when(tile > 0)
+        def _():
+            frames_copy(tile - 1, part).wait()
+
+        frames_part(part)
+        frames_copy(tile, part).start()
+
+        @pl.when((tile == last_tile) & (part == 0))
+        def _():
+            after_near()
+
+        @pl.when((tile == last_tile) & (part == 1))
+        def _():
+            after_far()
+
+        return carry
+
+    lax.fori_loop(0, 3, one_part, 0)
+
+    @pl.when(tile == last_tile)
+    def _():
         complete(last_phase)
         dense_copy().start()
         for k in range(1, 4):
@@ -1178,7 +1192,7 @@
     loss_scale,
     section_ref,
     frames_any,
-    dense_ref,
+    dense_any,
     sum_ref,
     own_ref,
     out_any,
@@ -1195,10 +1209,13 @@
     loss_ref,
     table_ref,
     buffer,
+    dense_ref,
+    dense_sem,
     in_sems,
     out_sems,
 ):
     step = pl.program_id(0)
+    dense_copy = pltpu.make_async_copy(dense_any, dense_ref, dense_sem)
     parts = in_sems.shape[0]
     part_rows = frames_any.shape[0] // parts
 
@@ -1214,8 +1231,7 @@
     def _():
         for k in range(parts):
             copy_in(k).start()
-        two_ref[0:464, :] = dense_ref[1568:2032, 0:256].astype(F32)
-        two_ref[464:918, :] = dense_ref[1568:2022, 256:512].astype(F32)
+        dense_copy.start()
         if owners == 16:
             mine = own_ref[pl.ds(pl.multiple_of(8 * section_ref[0], 8), 8), :]
             table_ref[0] = 0.5 * mine[:, 96 : 96 + table_ref.shape[2]]
@@ -1236,6 +1252,9 @@
         for k in range(parts):
             copy_in(k).wait()
             copy_out(k).start()
+        dense_copy.wait()
+        two_ref[0:464, :] = dense_ref[1568:2032, 0:256].astype(F32)
+        two_ref[464:918, :] = dense_ref[1568:2022, 256:512].astype(F32)
 
     at = pl.ds(pl.multiple_of(step * 784, 16), 784)
     one_ref[...] = dense_ref[at, :].astype(F32)
@@ -1254,7 +1273,7 @@
         in_specs=[
             pl.BlockSpec(memory_space=pltpu.SMEM),
             pl.BlockSpec(memory_space=pl.ANY),
-            whole(dense.shape),
+            pl.BlockSpec(memory_space=pl.ANY),
             whole(sums.shape),
             whole(own.shape),
         ],
@@ -1267,6 +1286,8 @@
         + [jax.ShapeDtypeStruct(a, F32) for a in others],
         scratch_shapes=[
             pltpu.VMEM(frames.shape, BF16),
+            pltpu.VMEM(dense.shape, BF16),
+            pltpu.SemaphoreType.DMA,
             pltpu.SemaphoreType.DMA((7,)),
             pltpu.SemaphoreType.DMA((7,)),
         ],

time: 130 us -> 131 us (level)
  no operation moved by 1% of the time
where the time goes in v2:
time: 131 us
  Pallas kernels  130 us (99%)
    pallas_call x1, Pallas kernels, backward(): pl.pallas_call(functools.partial(backward_kernel, capacity), grid=(lanes...  66.5 us
    pallas_call x1, Pallas kernels, head(): pl.pallas_call(head_kernel, grid=(2 * (lanes // LANES) - 1,), in_specs=[a...  51.2 us
    pallas_call x1, Pallas kernels, last(): pl.pallas_call(functools.partial(last_kernel, owners, 0.5 / (frames.shape...  12.1 us

profile of v2, /device:TPU:1, one launch (start us, length us, event | category | flops | bytes accessed | tf_op | source)
XLA Modules:
  0.0 130.6 jit_solution(12919016411942847353)
XLA Ops:
  0.7 51.2 %shard_map.399 = (bf16[3,20,640,128]{3,2,1,0:T(8,128)(2,1)}, bf16[3,20,640,128]{3,2,1,0:T(8,128)(2,1)}, bf16[3,9,576,128]{3,2,1,0:T(8,128)(2,1)}, bf16[3,9,576,1...) custom-call(bf16[84,84,4,384]{3,2,1,0:T(4,128)(2,1)} %bitcast.56, ...), custom_call_target="tpu_custom_call" | custom-call | flops 12525568000 | bytes 67108864 | tf_op jit(solution)/shard_map/pallas_call | solution.py:513
  51.9 66.5 %shard_map.400 = (bf16[84,84,2,384]{3,2,1,0:T(2,128)(2,1)}, bf16[2048,512]{1,0:T(8,128)(2,1)}, f32[16,32,128]{2,1,0:T(8,128)}, f32[32,128]{1,0:T(8,128)}) custom-call(bf16[3,9,576,128]{3,2,1,0:T(8,128)(2,1)} %get-tuple-element.42.a2_ref, bf16[3,9,576,128]{3,2,1,0:T(8,128)(2,1)} %get-tuple-element.43.s2_ref, ...), custom_call_target="tpu_custom_call" | custom-call | flops 8903983104 | bytes 65028096 | tf_op jit(solution)/shard_map/pallas_call | solution.py:1136
  118.4 12.1 %shard_map.401 = (bf16[84,84,2,384]{3,2,1,0:T(2,128)(2,1)}, f32[1568,512]{1,0:T(8,128)}, f32[918,256]{1,0:T(8,128)}, f32[256,16]{1,0:T(8,128)}, f32[512,32]{1,0:...) custom-call(s32[1]{0:T(128)} %bitcast.section_ref, ...), custom_call_target="tpu_custom_call" | custom-call | bytes 33554432 | tf_op jit(solution)/shard_map/pallas_call | solution.py:1270

commit v3 on v1

--- a/solution.py
+++ b/solution.py
@@ -256,9 +256,6 @@
         barrier = pltpu.get_barrier_semaphore()
         pl.semaphore_signal(barrier, inc=1, device_id=(1 - section, batch), device_id_type=MESH)
         start_x(step)
-        dense_copy(target_dense_any).start()
-
-    start_x(step + 1)
 
     def prepare(one_ref, two_ref, three_ref, off_one, off_two, off_three):
         wt1[...] = jnp.zeros_like(wt1)
@@ -319,6 +316,12 @@
         x_copy(x_any, tile, step, k).wait()
         in_turn([strips_one(i, s) for i in pairs for s in range(4)])
     start_outs((0, 1))
+    start_x(step + 1)
+
+    @pl.when(step == 0)
+    def _():
+        dense_copy(target_dense_any).start()
+
     wait_outs((2, 3, 4, 5))
 
     def strips_two(places):
@@ -531,14 +534,14 @@
     x_any,
     f_any,
     dense_weight_any,
+    p2_any,
+    q1_any,
     hg_ref,
     lg_ref,
     active_ref,
     w1_ref,
     w2_ref,
     w3_ref,
-    p2_ref,
-    q1_ref,
     owner_ref,
     loss_ref,
     sum1_ref,
@@ -567,6 +570,9 @@
     dense_sem,
     a1_ref,
     s1_ref,
+    p2_ref,
+    q1_ref,
+    choice_sems,
     xbuf,
     fbuf,
     dense_weight_ref,
@@ -748,21 +754,27 @@
         half = fbuf.shape[0]
         return pltpu.make_async_copy(f_any.at[rows_at(half * section, half), :], fbuf, f_sem)
 
+    def choice_copy(k):
+        source, into = ((p2_any, p2_ref), (q1_any, q1_ref))[k]
+        return pltpu.make_async_copy(source, into, choice_sems.at[k])
+
     def weight_copy():
         return pltpu.make_async_copy(dense_weight_any, dense_weight_ref, weight_sem)
 
     @pl.when(tile == 0)
     def _():
         f_copy().start()
-        weight_copy().start()
-        for k in range(2):
-            a_copy(tile, k).start()
         barrier = pltpu.get_barrier_semaphore()
         for k in range(1, 8):
             pl.semaphore_signal(barrier, inc=1, device_id=near(k)[1], device_id_type=MESH)
         for k in range(1, high_count):
             pl.semaphore_signal(barrier, inc=1, device_id=far(k)[1], device_id_type=MESH)
         f_copy().wait()
+        for k in range(2):
+            choice_copy(k).start()
+        weight_copy().start()
+        for k in range(2):
+            a_copy(tile, k).start()
 
         def dense_one(start, stop):
             for at in range(start, stop, 256):
@@ -806,6 +818,8 @@
                     ref[r, ref.shape[1] - edge * width :, :] = side
                 else:
                     ref[r] = jnp.zeros((ref.shape[1], LANES), BF16)
+        for k in range(2):
+            choice_copy(k).wait()
         rows = (0.5 * nn_dot(p2_ref[...], w2_ref[...])).astype(BF16)
         for dp in range(2):
             for dq in range(2):
@@ -1108,9 +1122,9 @@
             frames_copy(tile, part).wait()
 
 
-def backward(tiles, anys, hg, lg, active, w1, w2, w3, p2, q1, owners, owner_count, capacity, losses, sum1, sum2):
+def backward(tiles, anys, hg, lg, active, w1, w2, w3, owners, owner_count, capacity, losses, sum1, sum2):
     lanes = hg.shape[-1]
-    small = (hg, lg, active, w1, w2, w3, p2, q1, owners, losses, sum1, sum2)
+    small = (hg, lg, active, w1, w2, w3, owners, losses, sum1, sum2)
     totals = [(768, 160), (1024, 192), (1152, 256), (160, LANES), (3136, LANES), (512, LANES)]
     totals += [(576, LANES), (256, LANES)]
     pack_shape = (2 * SLICE * owner_count, LANES)
@@ -1141,6 +1155,9 @@
             pltpu.SemaphoreType.DMA,
             pltpu.VMEM((20, 640, LANES), BF16),
             pltpu.VMEM((20, 640, LANES), BF16),
+            pltpu.VMEM((512, 512), BF16),
+            pltpu.VMEM((16 * 224, 128), BF16),
+            pltpu.SemaphoreType.DMA((2,)),
             pltpu.VMEM((44, 336, LANES), BF16),
             pltpu.VMEM((1568, lanes), BF16),
             pltpu.VMEM((3136, 512), BF16),
@@ -1362,13 +1379,11 @@
     capacity = (rows + owner_count - 1) // owner_count + 1
     frames_grad, dense, sums, own = backward(
         (a2, s2, s3),
-        (a1, s1, x, feature, dense_one_weight),
+        (a1, s1, x, feature, dense_one_weight, p2, q1),
         hidden_grad,
         logit_grad,
         active,
         *online[:3],
-        p2,
-        q1,
         owners.T,
         owner_count,
         capacity,

time: 130 us -> 132 us (1.015)
  Pallas kernels: 129 us -> 131 us
    pallas_call x1, Pallas kernels: 51.1 us -> 53 us  [head(): pl.pallas_call(head_kernel, grid=(2 * (lanes // LANES) - 1,), in_specs=[a...]
where the time goes in v3:
time: 132 us
  Pallas kernels  131 us (99%)
    pallas_call x1, Pallas kernels, backward(): pl.pallas_call(functools.partial(backward_kernel, capacity), grid=(lanes...  66.7 us
    pallas_call x1, Pallas kernels, head(): pl.pallas_call(head_kernel, grid=(2 * (lanes // LANES) - 1,), in_specs=[a...  53 us
    pallas_call x1, Pallas kernels, last(): pl.pallas_call(functools.partial(last_kernel, owners, 0.5 / (frames.shape...  11.6 us

profile of v3, /device:TPU:1, one launch (start us, length us, event | category | flops | bytes accessed | tf_op | source)
XLA Modules:
  0.0 132.1 jit_solution(13225079867648498508)
XLA Ops:
  0.7 53.0 %shard_map.399 = (bf16[3,20,640,128]{3,2,1,0:T(8,128)(2,1)}, bf16[3,20,640,128]{3,2,1,0:T(8,128)(2,1)}, bf16[3,9,576,128]{3,2,1,0:T(8,128)(2,1)}, bf16[3,9,576,1...) custom-call(bf16[84,84,4,384]{3,2,1,0:T(4,128)(2,1)} %bitcast.56, ...), custom_call_target="tpu_custom_call" | custom-call | flops 12525568000 | bytes 67108864 | tf_op jit(solution)/shard_map/pallas_call | solution.py:503
  53.7 66.7 %shard_map.400 = (bf16[84,84,2,384]{3,2,1,0:T(2,128)(2,1)}, bf16[2048,512]{1,0:T(8,128)(2,1)}, f32[16,32,128]{2,1,0:T(8,128)}, f32[32,128]{1,0:T(8,128)}) custom-call(bf16[3,9,576,128]{3,2,1,0:T(8,128)(2,1)} %get-tuple-element.42.a2_ref, bf16[3,9,576,128]{3,2,1,0:T(8,128)(2,1)} %get-tuple-element.43.s2_ref, ...), custom_call_target="tpu_custom_call" | custom-call | flops 8903983104 | bytes 65028096 | tf_op jit(solution)/shard_map/pallas_call | solution.py:1136
  120.4 11.6 %shard_map.401 = (bf16[84,84,2,384]{3,2,1,0:T(2,128)(2,1)}, f32[1568,512]{1,0:T(8,128)}, f32[918,256]{1,0:T(8,128)}, f32[256,16]{1,0:T(8,128)}, f32[512,32]{1,0:...) custom-call(s32[1]{0:T(128)} %bitcast.section_ref, ...), custom_call_target="tpu_custom_call" | custom-call | bytes 33554432 | tf_op jit(solution)/shard_map/pallas_call | solution.py:1268

commit v4 on v3

--- a/solution.py
+++ b/solution.py
@@ -13,7 +13,7 @@
 NSTEP = 3
 LANES = 128
 SLICE = 32
-ROW_CHUNKS = ((0, 36), (36, 84))
+ROW_CHUNKS = ((0, 12), (12, 24), (24, 36), (36, 52), (52, 68), (68, 84))
 MESH = pl.DeviceIdType.MESH
 support_low = -10.0
 support_high = 10.0
@@ -256,6 +256,9 @@
         barrier = pltpu.get_barrier_semaphore()
         pl.semaphore_signal(barrier, inc=1, device_id=(1 - section, batch), device_id_type=MESH)
         start_x(step)
+        dense_copy(target_dense_any).start()
+
+    start_x(step + 1)
 
     def prepare(one_ref, two_ref, three_ref, off_one, off_two, off_three):
         wt1[...] = jnp.zeros_like(wt1)
@@ -313,15 +316,10 @@
 
     wait_outs((0, 1))
     for k, pairs in enumerate((range(0, 4), range(4, 10))):
-        x_copy(x_any, tile, step, k).wait()
+        for n in range(3 * k, 3 * k + 3):
+            x_copy(x_any, tile, step, n).wait()
         in_turn([strips_one(i, s) for i in pairs for s in range(4)])
     start_outs((0, 1))
-    start_x(step + 1)
-
-    @pl.when(step == 0)
-    def _():
-        dense_copy(target_dense_any).start()
-
     wait_outs((2, 3, 4, 5))
 
     def strips_two(places):

time: 132 us -> 130 us (0.985)
  Pallas kernels: 131 us -> 129 us
    pallas_call x1, Pallas kernels: 53 us -> 51.3 us  [head(): pl.pallas_call(head_kernel, grid=(2 * (lanes // LANES) - 1,), in_specs=[a...]
where the time goes in v4:
time: 130 us
  Pallas kernels  129 us (99%)
    pallas_call x1, Pallas kernels, backward(): pl.pallas_call(functools.partial(backward_kernel, capacity), grid=(lanes...  66.7 us
    pallas_call x1, Pallas kernels, head(): pl.pallas_call(head_kernel, grid=(2 * (lanes // LANES) - 1,), in_specs=[a...  51.3 us
    pallas_call x1, Pallas kernels, last(): pl.pallas_call(functools.partial(last_kernel, owners, 0.5 / (frames.shape...  11.6 us

profile of v4, /device:TPU:1, one launch (start us, length us, event | category | flops | bytes accessed | tf_op | source)
XLA Modules:
  0.0 130.3 jit_solution(1993187064083587584)
XLA Ops:
  0.7 51.3 %shard_map.399 = (bf16[3,20,640,128]{3,2,1,0:T(8,128)(2,1)}, bf16[3,20,640,128]{3,2,1,0:T(8,128)(2,1)}, bf16[3,9,576,128]{3,2,1,0:T(8,128)(2,1)}, bf16[3,9,576,1...) custom-call(bf16[84,84,4,384]{3,2,1,0:T(4,128)(2,1)} %bitcast.56, ...), custom_call_target="tpu_custom_call" | custom-call | flops 12525568000 | bytes 67108864 | tf_op jit(solution)/shard_map/pallas_call | solution.py:501
  51.9 66.7 %shard_map.400 = (bf16[84,84,2,384]{3,2,1,0:T(2,128)(2,1)}, bf16[2048,512]{1,0:T(8,128)(2,1)}, f32[16,32,128]{2,1,0:T(8,128)}, f32[32,128]{1,0:T(8,128)}) custom-call(bf16[3,9,576,128]{3,2,1,0:T(8,128)(2,1)} %get-tuple-element.42.a2_ref, bf16[3,9,576,128]{3,2,1,0:T(8,128)(2,1)} %get-tuple-element.43.s2_ref, ...), custom_call_target="tpu_custom_call" | custom-call | flops 8903983104 | bytes 65028096 | tf_op jit(solution)/shard_map/pallas_call | solution.py:1134
  118.6 11.6 %shard_map.401 = (bf16[84,84,2,384]{3,2,1,0:T(2,128)(2,1)}, f32[1568,512]{1,0:T(8,128)}, f32[918,256]{1,0:T(8,128)}, f32[256,16]{1,0:T(8,128)}, f32[512,32]{1,0:...) custom-call(s32[1]{0:T(128)} %bitcast.section_ref, ...), custom_call_target="tpu_custom_call" | custom-call | bytes 33554432 | tf_op jit(solution)/shard_map/pallas_call | solution.py:1266
